TPU v7x, 32 devices: a whole 2x2x4 slice. The times are simulated.
32 devices in a mesh: outer: 8 (over y, x, core), inner: 4 (over z).
Axes of the slice: x: 2, y: 2, z: 4, core: 2. Of those that a mesh axis runs over, the one named last changes fastest.
Arguments:
- queries: bfloat16 [4096, 1024], P(('outer', 'inner')), may hold values from -4.5 to 4.5
- key_vectors: bfloat16 [4096, 128], P(('outer', 'inner')), may hold values from -4.5 to 4.5
- value_vectors: bfloat16 [4096, 128], P(('outer', 'inner')), may hold values from -4 to 4
- grad_output: bfloat16 [4096, 1024], P(('outer', 'inner')), may hold values from -4 to 4
- positions: int32 [4096], P(('outer', 'inner')), may hold values from 0 to 4095, as said below
Outputs:
- attended: bfloat16 [4096, 1024], P(('outer', 'inner'))
- grad_queries: bfloat16 [4096, 1024], P(('outer', 'inner'))
- grad_keys: bfloat16 [4096, 128], P(('outer', 'inner'))
- grad_values: bfloat16 [4096, 128], P(('outer', 'inner'))
Inputs may be any that keep to these rules, and one draw needn't show every extreme that they name: Each run of 512 rows holds the positions of one segment, 512 times the segment's number plus 0 to 511, each once. The 128 rows of one device hold two blocks of 64 ascending consecutive positions: block b of its segment first, then block 7 - b, where b runs over a permutation of 0 to 3 drawn anew for each segment.
All inputs are finite; a program needn't handle non-finite values.
Results may differ from a plain program's by a relative error of at most 0.03.
Values may be sent and summed in bfloat16 or wider, within the bound.
A program may use at most 64 MiB of HBM per device.

v0:
```python
import jax
import jax.numpy as jnp
from jax import lax
from jax.sharding import PartitionSpec as P

masked_score = -1e30


def from_behind(block, axis, distance):
    devices = range(lax.axis_size(axis))
    route = [(i - distance, i) for i in devices if i - distance in devices]
    return lax.ppermute(block, axis, route)


def block_scores(query_block, key_block, score_scale):
    return (
        jnp.einsum("thd,kd->thk", query_block, key_block, preferred_element_type=jnp.float32)
        * score_scale
    )


def body(queries, key_vectors, value_vectors, grad_output, positions):
    tok_rows, full_width = queries.shape
    head_dim = key_vectors.shape[1]
    head_count = full_width // head_dim
    score_scale = float(head_dim) ** (-0.5)
    key_value = jnp.concatenate([key_vectors, value_vectors], axis=1)
    group_kv, group_positions = (
        lax.all_gather(key_value, "inner", axis=0, tiled=True),
        lax.all_gather(positions, "inner", axis=0, tiled=True),
    )
    prev_kv = from_behind(group_kv, "outer", 1)
    own_keys = group_kv[:, :head_dim]
    own_values = group_kv[:, head_dim:]
    prev_keys = prev_kv[:, :head_dim]
    prev_values = prev_kv[:, head_dim:]
    has_prev = lax.axis_index("outer") > 0
    own_mask = group_positions[None, :] <= positions[:, None]
    head_block = head_count
    while head_block * tok_rows > 512 and head_block % 2 == 0:
        head_block = head_block // 2
    span_rows = group_kv.shape[0]
    own_terms = jnp.zeros((span_rows, 2 * head_dim), jnp.float32)
    prev_terms = jnp.zeros((span_rows, 2 * head_dim), jnp.float32)
    attn_parts = []
    query_parts = []
    for head_start in range(0, head_count, head_block):
        col_start = head_start * head_dim
        col_stop = (head_start + head_block) * head_dim
        query_block = queries[:, col_start:col_stop].reshape(tok_rows, head_block, head_dim)
        grad_block = grad_output[:, col_start:col_stop].reshape(tok_rows, head_block, head_dim)
        own_scores = jnp.where(
            own_mask[:, None, :], block_scores(query_block, own_keys, score_scale), masked_score
        )
        prev_scores = jnp.where(
            has_prev, block_scores(query_block, prev_keys, score_scale), masked_score
        )
        row_max = jnp.maximum(
            jnp.max(own_scores, axis=-1, keepdims=True),
            jnp.max(prev_scores, axis=-1, keepdims=True),
        )
        own_exp = jnp.exp(own_scores - row_max)
        prev_exp = jnp.exp(prev_scores - row_max)
        row_total = jnp.sum(own_exp, axis=-1, keepdims=True) + jnp.sum(
            prev_exp, axis=-1, keepdims=True
        )
        own_probs = own_exp / row_total
        prev_probs = prev_exp / row_total
        own_weights = own_probs.astype(jnp.bfloat16)
        prev_weights = prev_probs.astype(jnp.bfloat16)
        attn_sum = jnp.einsum(
            "thk,kd->thd", own_weights, own_values, preferred_element_type=jnp.float32
        )
        attn_sum = attn_sum + jnp.einsum(
            "thk,kd->thd", prev_weights, prev_values, preferred_element_type=jnp.float32
        )
        attn_out = attn_sum.astype(jnp.bfloat16)
        row_delta = jnp.sum(
            grad_block.astype(jnp.float32) * attn_out.astype(jnp.float32), axis=-1, keepdims=True
        )
        own_pgrad = jnp.einsum(
            "thd,kd->thk", grad_block, own_values, preferred_element_type=jnp.float32
        )
        prev_pgrad = jnp.einsum(
            "thd,kd->thk", grad_block, prev_values, preferred_element_type=jnp.float32
        )
        own_dscore = (own_probs * (own_pgrad - row_delta)).astype(jnp.bfloat16)
        prev_dscore = (prev_probs * (prev_pgrad - row_delta)).astype(jnp.bfloat16)
        query_grad = jnp.einsum(
            "thk,kd->thd", own_dscore, own_keys, preferred_element_type=jnp.float32
        )
        query_grad = query_grad + jnp.einsum(
            "thk,kd->thd", prev_dscore, prev_keys, preferred_element_type=jnp.float32
        )
        query_grad = (query_grad * score_scale).astype(jnp.bfloat16)
        own_terms = own_terms + jnp.concatenate(
            [
                jnp.einsum(
                    "thk,thd->kd", own_dscore, query_block, preferred_element_type=jnp.float32
                )
                * score_scale,
                jnp.einsum(
                    "thk,thd->kd", own_weights, grad_block, preferred_element_type=jnp.float32
                ),
            ],
            axis=1,
        )
        prev_terms = prev_terms + jnp.concatenate(
            [
                jnp.einsum(
                    "thk,thd->kd", prev_dscore, query_block, preferred_element_type=jnp.float32
                )
                * score_scale,
                jnp.einsum(
                    "thk,thd->kd", prev_weights, grad_block, preferred_element_type=jnp.float32
                ),
            ],
            axis=1,
        )
        attn_parts.append(attn_out.reshape(tok_rows, head_block * head_dim))
        query_parts.append(query_grad.reshape(tok_rows, head_block * head_dim))
    attended = jnp.concatenate(attn_parts, axis=1)
    grad_queries = jnp.concatenate(query_parts, axis=1)
    returned = from_behind(prev_terms.astype(jnp.bfloat16), "outer", -1).astype(prev_terms.dtype)
    key_grads = lax.psum_scatter(
        (own_terms + returned).astype(jnp.bfloat16), "inner", scatter_dimension=0, tiled=True
    ).astype(jnp.float32)
    grad_keys = key_grads[:, :head_dim].astype(jnp.bfloat16)
    grad_values = key_grads[:, head_dim:].astype(jnp.bfloat16)
    return (attended, grad_queries, grad_keys, grad_values)


def solution(mesh):
    return jax.shard_map(
        body,
        mesh=mesh,
        in_specs=(
            P(("outer", "inner"), None),
            P(("outer", "inner"), None),
            P(("outer", "inner"), None),
            P(("outer", "inner"), None),
            P(("outer", "inner")),
        ),
        out_specs=(
            P(("outer", "inner"), None),
            P(("outer", "inner"), None),
            P(("outer", "inner"), None),
            P(("outer", "inner"), None),
        ),
        check_vma=False,
    )
```

profile of v0, /device:TPU:0, one launch (start us, length us, event | category | flops | bytes accessed | tf_op | source)
XLA Modules:
  0.0 81.0 jit_solution(5575179207128493894)
XLA Ops:
  7.2 0.0 copy-start
  7.2 0.0 reduce-scatter.4.cloned.1.call-start
  7.2 0.8 %pad_maximum_fusion.2 = bf16[128,256]{1,0:T(8,128)(2,1)S(1)} fusion(bf16[128,128]{1,0:T(8,128)(2,1)} %param.7, bf16[128,128]{1,0:T(8,128)(2,1)} %param.6), kind=kLoop, calls=%fused_computation.80 | loop fusion | flops 131072 | bytes 131072 | tf_op jit(solution)/shard_map/concatenate | solution.py:27
  8.0 15.6 %all_gather.7 = bf16[512,256]{1,0:T(8,128)(2,1)S(1)} all-gather(bf16[128,256]{1,0:T(8,128)(2,1)S(1)} %pad_maximum_fusion.2), channel_id=1, replica_groups=mesh['outer'=8,'inner'=4] {'inner'}, dimensions={0}, use_global_device_ids=true | all-gather | bytes 327680 | tf_op jit(solution)/shard_map/all_gather | solution.py:29
  23.7 0.0 copy-start.2
  23.7 1.4 %collective-permute-start = (bf16[512,256]{1,0:T(8,128)(2,1)S(1)}, bf16[512,256]{1,0:T(8,128)(2,1)S(1)}, u32[]{:S(2)}, u32[]{:S(2)}) collective-permute-start(bf16[512,256]{1,0:T(8,128)(2,1)S(1)} %all_gather.7), channel_id=1, source_target_pairs={{0,4},{4,8},{8,12},{12,16},{16,20},{20,24},{24,28},{1,5},{5,9},{9,... | collective-permute-start | bytes 786440 | tf_op jit(solution)/shard_map/ppermute | solution.py:12
  25.1 0.0 copy-done.2
  25.1 11.4 %all-gather = s32[4,1,128]{2,1,0:T(1,128)S(1)} all-gather(s32[1,1,128]{2,1,0:T(1,128)S(1)} %bitcast.170), channel_id=1, replica_groups=mesh['outer'=8,'inner'=4] {'inner'}, dimensions={0}, use_global_device_ids=true | all-gather | bytes 2560 | tf_op jit(solution)/shard_map/all_gather | solution.py:30
  36.5 0.1 broadcast_compare_fusion
  36.6 0.0 copy-done
  36.7 0.1 copy.176
  36.8 0.0 copy-start.1
  36.8 0.3 fusion.52
  37.1 0.6 copy-done.1
  37.8 0.1 copy.175
  37.9 0.1 copy.107
  38.0 0.1 copy.114
  38.2 0.3 fusion.54
  38.5 0.0 collective-permute-done
  38.5 0.3 fusion.55
  38.8 0.3 fusion.33
  39.1 0.3 fusion.43
  39.5 0.3 fusion.48
  39.7 0.3 convolution_bitcast_fusion.6
  40.1 0.3 convolution_bitcast_fusion.2
  40.4 0.3 multiply_reduce_fusion.1
  40.7 0.3 fusion.19
  41.0 0.3 fusion.23
  41.3 0.3 fusion.46
  41.6 0.3 fusion.18
  41.9 0.3 fusion.21
  42.2 0.3 fusion.53
  42.6 0.3 fusion.37
  42.9 0.4 fusion.41
  43.2 0.3 fusion.47
  43.5 0.3 convolution_bitcast_fusion
  43.8 0.3 multiply_reduce_fusion
  44.1 0.3 fusion.17
  44.4 0.3 fusion.16
  44.8 0.3 fusion.20
  45.1 0.1 fusion.40
  45.2 1.3 %collective-permute-start.1 = (bf16[512,256]{0,1:T(8,128)(2,1)S(1)}, bf16[512,256]{0,1:T(8,128)(2,1)}, u32[]{:S(2)}, u32[]{:S(2)}) collective-permute-start(bf16[512,256]{0,1:T(8,128)(2,1)S(1)} %fusion.40), channel_id=1, source_target_pairs={{4,0},{8,4},{12,8},{16,12},{20,16},{24,20},{28,24},{5,1},{9,5},{13... | collective-permute-start | bytes 786440 | tf_op jit(solution)/shard_map/ppermute | solution.py:12
  46.5 0.3 fusion.29
  46.8 0.3 convolution_bitcast_fusion.4
  47.1 0.1 copy.105
  47.2 0.1 copy.121
  47.4 0.1 copy.106
  47.5 0.3 fusion.22
  47.8 1.0 %collective-permute-done.1 = bf16[512,256]{0,1:T(8,128)(2,1)} collective-permute-done((bf16[512,256]{0,1:T(8,128)(2,1)S(1)}, bf16[512,256]{0,1:T(8,128)(2,1)}, u32[]{:S(2)}, u32[]{:S(2)}) %collective-permute-start.1) | collective-permute-done | bytes 262176 | tf_op jit(solution)/shard_map/ppermute | solution.py:12
  48.8 1.1 %fusion.39 = bf16[512,256]{0,1:T(8,128)(2,1)S(1)} fusion(f32[512,128]{0,1:T(8,128)S(1)} %convolution_bitcast_fusion.6, f32[512,128]{0,1:T(8,128)S(1)} %fusion.23, f32[512,128]{0,1:T(8,128)S(1)} %convolution_bitcast_fusion.4, f32[512,128]{0,1:T(8,128)S(1)} %fusion.22, bf16[512,256]{0,1:T(8,128)(2,1)} %collective-permute-done.1), kind=kLoop, calls=%fused_computation.64 | loop fusion | flops 786432 | bytes 1572864 | tf_op jit(solution)/shard_map/convert_element_type | solution.py:126
  49.9 0.8 %copy.173 = bf16[512,256]{1,0:T(8,128)(2,1)} copy(bf16[512,256]{0,1:T(8,128)(2,1)S(1)} %fusion.39) | data formatting | bytes 524288
  50.7 0.0 reduce-scatter.4.cloned.1.call-update
  50.7 0.3 fusion.45
  51.0 0.3 fusion.28
  51.3 0.1 copy.122
  51.4 0.9 %pad_maximum_fusion = (bf16[128,1024]{1,0:T(8,128)(2,1)}, bf16[128,1024]{1,0:T(8,128)(2,1)}) fusion(bf16[128,512]{1,0:T(8,128)(2,1)S(1)} %copy.106, bf16[128,512]{1,0:T(8,128)(2,1)S(1)} %copy.105, bf16[128,512]{1,0:T(8,128)(2,1)S(1)} %copy.122, bf16[128,512]{1,0:T(8,128)(2,1)S(1)} %copy.121), kind=kLoop, calls=%fused_computation.71 | loop fusion | flops 1048576 | bytes 1048576 | tf_op jit(solution)/shard_map/concatenate | solution.py:122
  52.3 20.5 %reduce-scatter.4.cloned.1.call-done = bf16[128,256]{1,0:T(8,128)(2,1)} async-done(((bf16[512,256]{1,0:T(8,128)(2,1)}), bf16[128,256]{1,0:T(8,128)(2,1)}) %reduce-scatter.4.cloned.1.call-update) | async-done | bytes 65552
  72.7 1.4 %fusion.51 = (bf16[128,128]{1,0:T(8,128)(2,1)}, bf16[128,128]{1,0:T(8,128)(2,1)}) fusion(bf16[128,256]{1,0:T(8,128)(2,1)} %reduce-scatter.4.cloned.1.call-done), kind=kLoop, calls=%fused_computation.87 | loop fusion | bytes 131072 | tf_op jit(solution)/shard_map/slice | solution.py:129
  (6 shorter events, 0.1 us)
Async XLA Ops:
  7.2 29.5 %copy-start = (bf16[128,1024]{1,0:T(8,128)(2,1)S(1)}, bf16[128,1024]{1,0:T(8,128)(2,1)}, u32[]{:S(2)}) copy-start(bf16[128,1024]{1,0:T(8,128)(2,1)} %param.5) | copy-start | bytes 786436
  7.2 65.6 %reduce-scatter.4.cloned.1.call-start = ((), (), s32[]{:S(2)}) async-start(), calls=%async_computation.1 | async-start | bytes 327680
  23.7 1.4 %copy-start.2 = (s32[128]{0:T(128)S(1)}, s32[128]{0:T(128)}, u32[]{:S(2)}) copy-start(s32[128]{0:T(128)} %param.9) | copy-start | bytes 1540
  23.7 14.8 %collective-permute-start = (bf16[512,256]{1,0:T(8,128)(2,1)S(1)}, bf16[512,256]{1,0:T(8,128)(2,1)S(1)}, u32[]{:S(2)}, u32[]{:S(2)}) collective-permute-start(bf16[512,256]{1,0:T(8,128)(2,1)S(1)} %all_gather.7), channel_id=1, source_target_pairs={{0,4},{4,8},{8,12},{12,16},{16,20},{20,24},{24,28},{1,5},{5,9},{9,... | collective-permute-start | bytes 786440 | tf_op jit(solution)/shard_map/ppermute | solution.py:12
  36.8 1.0 %copy-start.1 = (bf16[128,1024]{1,0:T(8,128)(2,1)S(1)}, bf16[128,1024]{1,0:T(8,128)(2,1)}, u32[]{:S(2)}) copy-start(bf16[128,1024]{1,0:T(8,128)(2,1)} %param.8) | copy-start | bytes 786436
  45.2 3.6 %collective-permute-start.1 = (bf16[512,256]{0,1:T(8,128)(2,1)S(1)}, bf16[512,256]{0,1:T(8,128)(2,1)}, u32[]{:S(2)}, u32[]{:S(2)}) collective-permute-start(bf16[512,256]{0,1:T(8,128)(2,1)S(1)} %fusion.40), channel_id=1, source_target_pairs={{4,0},{8,4},{12,8},{16,12},{20,16},{24,20},{28,24},{5,1},{9,5},{13... | collective-permute-start | bytes 786440 | tf_op jit(solution)/shard_map/ppermute | solution.py:12
Sparse Core Ops, SparseCore 0:
  50.8 21.8 reduce-scatter.3
where the time goes:
time: 81.3 us; the launch traced here: 81 us
  blocking collectives  27 us (33%)
  waiting for transfers between devices  21.5 us (26%)
  between operations  14.4 us (18%)
  matrix products  7.18 us (9%)
  other arithmetic  4.33 us (5%)
  local copies, waits for them, and re-layouts  3.86 us (5%)
  starting transfers between devices  2.76 us (3%)
    unnamed x2, waiting for transfers between devices  20.5 us
    all_gather x1, blocking collectives, body(): lax.all_gather(key_value, 'inner', axis=0, tiled=True)  15.6 us
    all_gather x1, blocking collectives, body(): lax.all_gather(positions, 'inner', axis=0, tiled=True)  11.4 us
    ppermute x2, starting transfers between devices, from_behind(): return lax.ppermute(block, axis, route)  2.72 us
    unnamed x9, local copies, waits for them, and re-layouts  1.72 us
  transfers between devices with their start and end apart: 3, of which 2 were waited for; matrix products, arithmetic and copies ran while one was open for 5% of the time, Pallas kernels for 0%

commit v1 on v0

v1 whole, which is shorter than its diff:
```python
import functools
import math

import jax
import jax.numpy as jnp
from jax import lax
from jax.experimental import pallas as pl
from jax.experimental.pallas import tpu as pltpu
from jax.sharding import PartitionSpec as P

masked_score = -1e30
MESH = pl.DeviceIdType.MESH
F32 = jnp.float32
BF16 = jnp.bfloat16


def dot_nt(a, b):
    return lax.dot_general(a, b, (((1,), (1,)), ((), ())), preferred_element_type=F32)


def dot_nn(a, b):
    return lax.dot_general(a, b, (((1,), (0,)), ((), ())), preferred_element_type=F32)


def kernel(
    segments, group, heads, dim, tok,
    q_ref, k_ref, v_ref, do_ref, pos_ref,
    att_ref, gq_ref, gk_ref, gv_ref,
    kv_own, kv_prev, qs, dos, q_t, do_t, s_ref, dp_ref, w_ref, g_send, g_recv, g_mine,
    kv_ssem, kv_rsem, g_ssem, g_rsem,
):
    seg = lax.axis_index("outer")
    me = lax.axis_index("inner")
    nxt = lax.rem(seg + 1, segments)
    prv = lax.rem(seg + segments - 1, segments)
    scale = float(dim) ** -0.5
    blocks = 2 * group

    barrier = pltpu.get_barrier_semaphore()
    partners = [(seg, lax.rem(me + d, group)) for d in range(1, group)]
    partners += [(nxt, lax.rem(me + d, group)) for d in range(group)]
    partners += [(prv, lax.rem(me + d, group)) for d in range(group)]
    for partner in partners:
        pl.semaphore_signal(barrier, inc=1, device_id=partner, device_id_type=MESH)

    pos = pos_ref[...]
    pos_hi = jnp.broadcast_to((pos >> 7).astype(F32), (8, tok))
    pos_lo = jnp.broadcast_to((pos & 127).astype(F32), (8, tok))
    kv_own[0, 0:tok, :] = k_ref[...]
    kv_own[0, tok : 2 * tok, :] = v_ref[...]
    kv_own[0, 2 * tok :, :] = jnp.concatenate([pos_hi, pos_lo], axis=0).astype(BF16)
    pl.semaphore_wait(barrier, len(partners))

    def kv_copy(block):
        d = block % group
        target = lax.rem(me + group - d, group)
        if block < group:
            src, dst, to = kv_own.at[0], kv_own.at[d], (seg, target)
        else:
            src, dst, to = kv_own.at[0, pl.ds(0, 2 * tok)], kv_prev.at[d], (nxt, target)
        return pltpu.make_async_remote_copy(
            src_ref=src, dst_ref=dst, send_sem=kv_ssem.at[block], recv_sem=kv_rsem.at[block],
            device_id=to, device_id_type=MESH,
        )

    kv_copies = {b: kv_copy(b) for b in range(1, blocks)}
    order = [group]
    for d in range(1, group):
        order += [d, group + d]
    for b in order:
        kv_copies[b].start()

    for h in range(heads):
        rows, cols = slice(h * tok, (h + 1) * tok), slice(h * dim, (h + 1) * dim)
        q_h, do_h = q_ref[:, cols], do_ref[:, cols]
        qs[rows, :] = q_h
        dos[rows, :] = do_h
        q_t[:, rows] = q_h.astype(F32).T.astype(BF16)
        do_t[:, rows] = do_h.astype(F32).T.astype(BF16)

    pos_col = jnp.broadcast_to(pos.astype(F32), (tok, tok)).T
    prev_bias = jnp.where(seg > 0, 0.0, masked_score).astype(F32)

    def keys_of(block):
        if block < group:
            return kv_own[block, 0:tok, :]
        return kv_prev[block - group, 0:tok, :]

    def values_of(block):
        if block < group:
            return kv_own[block, tok : 2 * tok, :]
        return kv_prev[block - group, tok : 2 * tok, :]

    def bias_of(block):
        if block >= group:
            return jnp.broadcast_to(prev_bias, (tok, tok))
        coded = kv_own[block, 2 * tok :, :].astype(F32)
        key_pos = coded[0:1, :] * 128.0 + coded[8:9, :]
        return jnp.where(key_pos <= pos_col, 0.0, masked_score)

    def cat(parts, axis):
        return parts[0] if len(parts) == 1 else jnp.concatenate(parts, axis=axis)

    steps = [[0], [1]] + [[b, b + 1] for b in range(2, blocks, 2)]
    for step in steps:
        for b in step:
            if b > 0:
                kv_copies[b].wait_recv()
        cols = slice(step[0] * tok, (step[-1] + 1) * tok)
        width = len(step) * tok
        score = dot_nt(qs[...], cat([keys_of(b) for b in step], 0))
        bias = cat([bias_of(b) for b in step], 1)
        score = score.reshape(heads, tok, width) + bias[None]
        s_ref[:, cols] = score.reshape(heads * tok, width)
        dp_ref[:, cols] = dot_nt(dos[...], cat([values_of(b) for b in step], 0))

    rate = scale * math.log2(math.e)
    for h in range(heads):
        rows = slice(h * tok, (h + 1) * tok)
        s = s_ref[rows, :]
        top = jnp.max(s, axis=1, keepdims=True)
        e = jnp.exp2((s - top) * rate)
        inv = 1.0 / jnp.sum(e, axis=1, keepdims=True)
        w_ref[rows, :] = (e * inv).astype(BF16)

    def grad_copy(block, part):
        d = block % group
        to = (seg if block < group else prv, lax.rem(me + d, group))
        return pltpu.make_async_remote_copy(
            src_ref=g_send.at[block, part], dst_ref=g_recv.at[block, part],
            send_sem=g_ssem.at[block, part], recv_sem=g_rsem.at[block, part],
            device_id=to, device_id_type=MESH,
        )

    grad_copies = {(b, p): grad_copy(b, p) for b in range(1, blocks) for p in range(2)}

    def send_grad(part, first, total):
        for n in range(2):
            b = first + n
            block = total[:, n * tok : (n + 1) * tok]
            if b == 0:
                g_mine[part] = block
            else:
                g_send[b, part] = block.astype(BF16)
                grad_copies[b, part].start()

    pairs = list(range(group, blocks, 2)) + list(range(group - 2, -1, -2))
    for first in pairs:
        cols = slice(first * tok, (first + 2) * tok)
        send_grad(1, first, dot_nn(do_t[...], w_ref[:, cols]))

    all_values = cat([values_of(b) for b in range(blocks)], 0)
    attended = dot_nn(w_ref[...], all_values).astype(BF16)
    delta = jnp.sum(dos[...].astype(F32) * attended.astype(F32), axis=1, keepdims=True)

    for first in pairs:
        cols = slice(first * tok, (first + 2) * tok)
        ds = (w_ref[:, cols].astype(F32) * (dp_ref[:, cols] - delta)).astype(BF16)
        w_ref[:, cols] = ds
        send_grad(0, first, dot_nn(q_t[...], ds) * scale)

    for h in range(heads):
        att_ref[:, h * dim : (h + 1) * dim] = attended[h * tok : (h + 1) * tok]

    all_keys = cat([keys_of(b) for b in range(blocks)], 0)
    gq = (dot_nn(w_ref[...], all_keys) * scale).astype(BF16)
    for h in range(heads):
        gq_ref[:, h * dim : (h + 1) * dim] = gq[h * tok : (h + 1) * tok]

    for part, out in ((1, gv_ref), (0, gk_ref)):
        total = g_mine[part]
        for b in range(1, blocks):
            grad_copies[b, part].wait_recv()
            total = total + g_recv[b, part].astype(F32)
        out[...] = total.T.astype(BF16)

    for b in range(1, blocks):
        kv_copies[b].wait_send()
        for part in range(2):
            grad_copies[b, part].wait_send()


def solution(mesh):
    segments, group = mesh.shape["outer"], mesh.shape["inner"]

    def body(queries, key_vectors, value_vectors, grad_output, positions):
        tok, full = queries.shape
        dim = key_vectors.shape[1]
        heads = full // dim
        blocks, rows = 2 * group, heads * tok
        keys = blocks * tok
        scratch = [
            ((group, 2 * tok + 16, dim), BF16),
            ((group, 2 * tok, dim), BF16),
            ((rows, dim), BF16),
            ((rows, dim), BF16),
            ((dim, rows), BF16),
            ((dim, rows), BF16),
            ((rows, keys), F32),
            ((rows, keys), F32),
            ((rows, keys), BF16),
            ((blocks, 2, dim, tok), BF16),
            ((blocks, 2, dim, tok), BF16),
            ((2, dim, tok), F32),
        ]
        used = sum(math.prod(s) * jnp.dtype(t).itemsize for s, t in scratch)
        vmem = pl.BlockSpec(memory_space=pltpu.VMEM)
        return pl.pallas_call(
            functools.partial(kernel, segments, group, heads, dim, tok),
            out_shape=[
                jax.ShapeDtypeStruct(queries.shape, BF16),
                jax.ShapeDtypeStruct(queries.shape, BF16),
                jax.ShapeDtypeStruct(key_vectors.shape, BF16),
                jax.ShapeDtypeStruct(key_vectors.shape, BF16),
            ],
            in_specs=[vmem] * 5,
            out_specs=[vmem] * 4,
            scratch_shapes=[pltpu.VMEM(s, t) for s, t in scratch]
            + [
                pltpu.SemaphoreType.DMA((blocks,)),
                pltpu.SemaphoreType.DMA((blocks,)),
                pltpu.SemaphoreType.DMA((blocks, 2)),
                pltpu.SemaphoreType.DMA((blocks, 2)),
            ],
            compiler_params=pltpu.CompilerParams(
                collective_id=0, has_side_effects=True, vmem_limit_bytes=used + (12 << 20)
            ),
            name="window_attention",
        )(queries, key_vectors, value_vectors, grad_output, positions.reshape(1, tok))

    rows = P(("outer", "inner"), None)
    return jax.shard_map(
        body,
        mesh=mesh,
        in_specs=(rows, rows, rows, rows, P(("outer", "inner"))),
        out_specs=(rows, rows, rows, rows),
        check_vma=False,
    )
```

time: 81.3 us -> 41 us (0.50)
  Pallas kernels: 0 us -> 33.3 us
  blocking collectives: 27 us -> 0 us
  waiting for transfers between devices: 21.5 us -> 0 us
  between operations: 14.4 us -> 0.65 us
  matrix products: 7.18 us -> 0 us
  other arithmetic: 4.33 us -> 0 us
  local copies, waits for them, and re-layouts: 3.86 us -> 6.7 us
  starting transfers between devices: 2.76 us -> 0 us
    pallas_call x0 -> x1, Pallas kernels: none -> 33.3 us  [body(): pl.pallas_call(functools.partial(kernel, segments, group, heads, dim, tok...]
    all_gather x2 -> x0, blocking collectives: 27 us -> none  [the longest x1 15.6 us: body(): lax.all_gather(key_value, 'inner', axis=0, tiled=True)]
    unnamed x2 -> x0, waiting for transfers between devices: 20.5 us -> none
    dot_general x24 -> x0, matrix products: 7.18 us -> none  [the longest x4 1.18 us: block_scores(): jnp.einsum('thd,kd->thk', query_block, key_block, preferred_element_type=...]
    unnamed x9 -> x14, local copies, waits for them, and re-layouts: 1.72 us -> 6.7 us
    ppermute x2 -> x0, starting transfers between devices: 2.72 us -> none  [from_behind(): return lax.ppermute(block, axis, route)]
    convert_element_type x4 -> x0, other arithmetic: 1.9 us -> none  [the longest x1 1.08 us: body(): (own_terms + returned).astype(jnp.bfloat16)]
    slice x5 -> x0, local copies, waits for them, and re-layouts: 1.68 us -> none  [the longest x1 1.4 us: body(): grad_values = key_grads[:, head_dim:].astype(jnp.bfloat16)]
  transfers between devices with their start and end apart: 3 -> 0, of which waited for: 2 -> 0; matrix products, arithmetic and copies ran while one was open for 5% -> 0% of each run, Pallas kernels for 0% -> 0%
where the time goes in v1:
time: 41 us; the launch traced here: 40.7 us
  Pallas kernels  33.3 us (81%)
  local copies, waits for them, and re-layouts  6.7 us (16%)
  between operations  0.65 us (2%)
    pallas_call x1, Pallas kernels, body(): pl.pallas_call(functools.partial(kernel, segments, group, heads, dim, tok...  33.3 us
    unnamed x14, local copies, waits for them, and re-layouts  6.7 us

profile of v1, /device:TPU:0, one launch (start us, length us, event | category | flops | bytes accessed | tf_op | source)
XLA Modules:
  0.0 40.7 jit_solution(17432528628510979017)
XLA Ops:
  0.6 0.0 copy-start.4
  0.6 0.6 %copy-done.4 = s32[128]{0:T(128)S(1)} copy-done((s32[128]{0:T(128)S(1)}, s32[128]{0:T(128)}, u32[]{:S(2)}) %copy-start.4) | copy-done | bytes 536
  1.3 0.0 copy-start
  1.3 0.9 %copy-done = bf16[128,1024]{1,0:T(8,128)(2,1)S(1)} copy-done((bf16[128,1024]{1,0:T(8,128)(2,1)S(1)}, bf16[128,1024]{1,0:T(8,128)(2,1)}, u32[]{:S(2)}) %copy-start) | copy-done | bytes 262168
  2.2 0.0 copy-start.1
  2.2 0.9 %copy-done.1 = bf16[128,1024]{1,0:T(8,128)(2,1)S(1)} copy-done((bf16[128,1024]{1,0:T(8,128)(2,1)S(1)}, bf16[128,1024]{1,0:T(8,128)(2,1)}, u32[]{:S(2)}) %copy-start.1) | copy-done | bytes 262168
  3.2 0.0 copy-start.2
  3.2 0.8 %copy-done.2 = bf16[128,128]{1,0:T(8,128)(2,1)S(1)} copy-done((bf16[128,128]{1,0:T(8,128)(2,1)S(1)}, bf16[128,128]{1,0:T(8,128)(2,1)}, u32[]{:S(2)}) %copy-start.2) | copy-done | bytes 32792
  3.9 0.0 copy-start.3
  4.0 0.8 %copy-done.3 = bf16[128,128]{1,0:T(8,128)(2,1)S(1)} copy-done((bf16[128,128]{1,0:T(8,128)(2,1)S(1)}, bf16[128,128]{1,0:T(8,128)(2,1)}, u32[]{:S(2)}) %copy-start.3) | copy-done | bytes 32792
  4.7 33.3 %window_attention.1 = (bf16[128,1024]{1,0:T(8,128)(2,1)S(1)}, bf16[128,1024]{1,0:T(8,128)(2,1)S(1)}, bf16[128,128]{1,0:T(8,128)(2,1)S(1)}, bf16[128,128]{1,0:T(8,128)(2,1)S(1)}) custom-call(bf16[128,1024]{1,0:T(8,128)(2,1)S(1)} %copy-done, bf16[128,128]{1,0:T(8,128)(2,1)S(1)} %copy-done.2, bf16[128,128]{1,0:T(8,128)(2,1)S(1)} %copy-done.3, ...), custom_call_target="tpu_custom_call" | custom-call | tf_op jit(solution)/shard_map/window_attention/pallas_call | solution.py:208
  38.1 0.7 %copy.13 = bf16[128,1024]{1,0:T(8,128)(2,1)} copy(bf16[128,1024]{1,0:T(8,128)(2,1)S(1)} %get-tuple-element.8) | data formatting | bytes 524288
  38.8 0.7 %copy.14 = bf16[128,1024]{1,0:T(8,128)(2,1)} copy(bf16[128,1024]{1,0:T(8,128)(2,1)S(1)} %get-tuple-element.9) | data formatting | bytes 524288
  39.5 0.6 %copy.15 = bf16[128,128]{1,0:T(8,128)(2,1)} copy(bf16[128,128]{1,0:T(8,128)(2,1)S(1)} %get-tuple-element.10) | data formatting | bytes 65536
  40.1 0.6 %copy.16 = bf16[128,128]{1,0:T(8,128)(2,1)} copy(bf16[128,128]{1,0:T(8,128)(2,1)S(1)} %get-tuple-element.11) | data formatting | bytes 65536
Async XLA Ops:
  0.6 0.7 %copy-start.4 = (s32[128]{0:T(128)S(1)}, s32[128]{0:T(128)}, u32[]{:S(2)}) copy-start(s32[128]{0:T(128)} %param.9) | copy-start | bytes 1540
  1.3 0.9 %copy-start = (bf16[128,1024]{1,0:T(8,128)(2,1)S(1)}, bf16[128,1024]{1,0:T(8,128)(2,1)}, u32[]{:S(2)}) copy-start(bf16[128,1024]{1,0:T(8,128)(2,1)} %q_ref.1) | copy-start | bytes 786436
  2.2 0.9 %copy-start.1 = (bf16[128,1024]{1,0:T(8,128)(2,1)S(1)}, bf16[128,1024]{1,0:T(8,128)(2,1)}, u32[]{:S(2)}) copy-start(bf16[128,1024]{1,0:T(8,128)(2,1)} %do_ref.1) | copy-start | bytes 786436
  3.2 0.8 %copy-start.2 = (bf16[128,128]{1,0:T(8,128)(2,1)S(1)}, bf16[128,128]{1,0:T(8,128)(2,1)}, u32[]{:S(2)}) copy-start(bf16[128,128]{1,0:T(8,128)(2,1)} %k_ref.1) | copy-start | bytes 98308
  3.9 0.8 %copy-start.3 = (bf16[128,128]{1,0:T(8,128)(2,1)S(1)}, bf16[128,128]{1,0:T(8,128)(2,1)}, u32[]{:S(2)}) copy-start(bf16[128,128]{1,0:T(8,128)(2,1)} %v_ref.1) | copy-start | bytes 98308

commit v2 on v1

v2 whole, which is shorter than its diff:
```python
import functools
import math

import jax
import jax.numpy as jnp
from jax import lax
from jax.experimental import pallas as pl
from jax.experimental.pallas import tpu as pltpu
from jax.sharding import PartitionSpec as P

masked_score = -1e30
vmem_bytes = (64 << 20) - (600 << 10)
MESH = pl.DeviceIdType.MESH
F32 = jnp.float32
BF16 = jnp.bfloat16


def dot_nt(a, b):
    return lax.dot_general(a, b, (((1,), (1,)), ((), ())), preferred_element_type=F32)


def dot_nn(a, b):
    return lax.dot_general(a, b, (((1,), (0,)), ((), ())), preferred_element_type=F32)


def kernel(
    segments, group, heads, dim, tok,
    q_hbm, k_hbm, v_hbm, do_hbm, pos_hbm,
    att_hbm, gq_hbm, gk_hbm, gv_hbm,
    q_ref, do_ref, pos_ref, kv_own, kv_prev, qs, dos, q_t, do_t, s_ref, dp_ref, w_ref,
    p_send, p_recv, g_send, g_recv, g_mine, att_ref, gq_ref, gk_ref, gv_ref,
    in_sem, out_sem, kv_ssem, kv_rsem, fw_ssem, fw_rsem, p_ssem, p_rsem, g_ssem, g_rsem,
):
    seg = lax.axis_index("outer")
    me = lax.axis_index("inner")
    nxt = lax.rem(seg + 1, segments)
    prv = lax.rem(seg + segments - 1, segments)
    scale = float(dim) ** -0.5
    blocks = 2 * group

    loads = [
        pltpu.make_async_copy(k_hbm, kv_own.at[0, pl.ds(0, tok)], in_sem.at[0]),
        pltpu.make_async_copy(v_hbm, kv_own.at[0, pl.ds(tok, tok)], in_sem.at[1]),
        pltpu.make_async_copy(pos_hbm, pos_ref, in_sem.at[2]),
        pltpu.make_async_copy(q_hbm, q_ref, in_sem.at[3]),
        pltpu.make_async_copy(do_hbm, do_ref, in_sem.at[4]),
    ]
    stores = [
        pltpu.make_async_copy(att_ref, att_hbm, out_sem.at[0]),
        pltpu.make_async_copy(gq_ref, gq_hbm, out_sem.at[1]),
        pltpu.make_async_copy(gk_ref, gk_hbm, out_sem.at[2]),
        pltpu.make_async_copy(gv_ref, gv_hbm, out_sem.at[3]),
    ]
    for load in loads:
        load.start()

    barrier = pltpu.get_barrier_semaphore()
    partners = [(seg, lax.rem(me + d, group)) for d in range(1, group)] + [(nxt, me), (prv, me)]
    for partner in partners:
        pl.semaphore_signal(barrier, inc=1, device_id=partner, device_id_type=MESH)

    for load in loads[:3]:
        load.wait()
    pos = pos_ref[...]
    pos_hi = jnp.broadcast_to((pos >> 7).astype(F32), (8, tok))
    pos_lo = jnp.broadcast_to((pos & 127).astype(F32), (8, tok))
    kv_own[0, 2 * tok :, :] = jnp.concatenate([pos_hi, pos_lo], axis=0).astype(BF16)
    pl.semaphore_wait(barrier, len(partners))

    def kv_copy(d):
        return pltpu.make_async_remote_copy(
            src_ref=kv_own.at[0], dst_ref=kv_own.at[d],
            send_sem=kv_ssem.at[d], recv_sem=kv_rsem.at[d],
            device_id=(seg, lax.rem(me + group - d, group)), device_id_type=MESH,
        )

    def kv_forward(d):
        return pltpu.make_async_remote_copy(
            src_ref=kv_own.at[d, pl.ds(0, 2 * tok)], dst_ref=kv_prev.at[d],
            send_sem=fw_ssem.at[d], recv_sem=fw_rsem.at[d],
            device_id=(nxt, me), device_id_type=MESH,
        )

    kv_copies = {d: kv_copy(d) for d in range(1, group)}
    kv_forwards = [kv_forward(d) for d in range(group)]
    for d in range(1, group):
        kv_copies[d].start()
    kv_forwards[0].start()

    for load in loads[3:]:
        load.wait()
    for h in range(heads):
        rows, cols = slice(h * tok, (h + 1) * tok), slice(h * dim, (h + 1) * dim)
        q_h, do_h = q_ref[:, cols], do_ref[:, cols]
        qs[rows, :] = q_h
        dos[rows, :] = do_h
        q_t[:, rows] = q_h.astype(F32).T.astype(BF16)
        do_t[:, rows] = do_h.astype(F32).T.astype(BF16)

    pos_col = jnp.broadcast_to(pos.astype(F32), (tok, tok)).T
    prev_bias = jnp.where(seg > 0, 0.0, masked_score).astype(F32)

    def keys_of(block):
        if block < group:
            return kv_own[block, 0:tok, :]
        return kv_prev[block - group, 0:tok, :]

    def values_of(block):
        if block < group:
            return kv_own[block, tok : 2 * tok, :]
        return kv_prev[block - group, tok : 2 * tok, :]

    def bias_of(block):
        if block >= group:
            return jnp.broadcast_to(prev_bias, (tok, tok))
        coded = kv_own[block, 2 * tok :, :].astype(F32)
        key_pos = coded[0:1, :] * 128.0 + coded[8:9, :]
        return jnp.where(key_pos <= pos_col, 0.0, masked_score)

    def cat(parts, axis):
        return parts[0] if len(parts) == 1 else jnp.concatenate(parts, axis=axis)

    def score_step(step):
        cols = slice(step[0] * tok, (step[-1] + 1) * tok)
        width = len(step) * tok
        score = dot_nt(qs[...], cat([keys_of(b) for b in step], 0))
        bias = cat([bias_of(b) for b in step], 1)
        score = score.reshape(heads, tok, width) + bias[None]
        s_ref[:, cols] = score.reshape(heads * tok, width)
        dp_ref[:, cols] = dot_nt(dos[...], cat([values_of(b) for b in step], 0))

    score_step([0])
    for d in range(1, group):
        kv_copies[d].wait_recv()
        kv_forwards[d].start()
        if d == 1:
            score_step([1])
        elif d % 2 == 1:
            score_step([d - 1, d])
    for d in range(0, group, 2):
        kv_forwards[d].wait_recv()
        kv_forwards[d + 1].wait_recv()
        score_step([group + d, group + d + 1])

    rate = scale * math.log2(math.e)
    for h in range(heads):
        rows = slice(h * tok, (h + 1) * tok)
        s = s_ref[rows, :]
        top = jnp.max(s, axis=1, keepdims=True)
        e = jnp.exp2((s - top) * rate)
        inv = 1.0 / jnp.sum(e, axis=1, keepdims=True)
        w_ref[rows, :] = (e * inv).astype(BF16)

    def prev_copy(part, first):
        return pltpu.make_async_remote_copy(
            src_ref=p_send.at[part, pl.ds(first, 2)], dst_ref=p_recv.at[part, pl.ds(first, 2)],
            send_sem=p_ssem.at[part, first], recv_sem=p_rsem.at[part, first],
            device_id=(prv, me), device_id_type=MESH,
        )

    def grad_copy(part, d):
        return pltpu.make_async_remote_copy(
            src_ref=g_send.at[part, d], dst_ref=g_recv.at[part, d],
            send_sem=g_ssem.at[part, d], recv_sem=g_rsem.at[part, d],
            device_id=(seg, lax.rem(me + d, group)), device_id_type=MESH,
        )

    firsts = list(range(0, group, 2))
    prev_copies = {(p, f): prev_copy(p, f) for p in range(2) for f in firsts}
    grad_copies = {(p, d): grad_copy(p, d) for p in range(2) for d in range(1, group)}

    def columns(first):
        return slice(first * tok, (first + 2) * tok)

    def send_prev(part, first, total):
        for n in range(2):
            p_send[part, first + n] = total[:, n * tok : (n + 1) * tok].astype(BF16)
        prev_copies[part, first].start()

    def send_own(part, first, total):
        prev_copies[part, first].wait_recv()
        for n in (1, 0):
            d = first + n
            block = total[:, n * tok : (n + 1) * tok] + p_recv[part, d].astype(F32)
            if d == 0:
                g_mine[part] = block
            else:
                g_send[part, d] = block.astype(BF16)
                grad_copies[part, d].start()

    def key_terms(first):
        cols = columns(first)
        ds = (w_ref[:, cols].astype(F32) * (dp_ref[:, cols] - delta)).astype(BF16)
        w_ref[:, cols] = ds
        return dot_nn(q_t[...], ds) * scale

    for first in firsts:
        send_prev(1, first, dot_nn(do_t[...], w_ref[:, columns(group + first)]))

    all_values = cat([values_of(b) for b in range(blocks)], 0)
    attended = dot_nn(w_ref[...], all_values).astype(BF16)
    delta = jnp.sum(dos[...].astype(F32) * attended.astype(F32), axis=1, keepdims=True)
    for h in range(heads):
        att_ref[:, h * dim : (h + 1) * dim] = attended[h * tok : (h + 1) * tok]
    stores[0].start()

    for first in firsts[::-1]:
        send_own(1, first, dot_nn(do_t[...], w_ref[:, columns(first)]))
    for first in firsts:
        send_prev(0, first, key_terms(group + first))
    for first in firsts[::-1]:
        send_own(0, first, key_terms(first))

    all_keys = cat([keys_of(b) for b in range(blocks)], 0)
    gq = (dot_nn(w_ref[...], all_keys) * scale).astype(BF16)
    for h in range(heads):
        gq_ref[:, h * dim : (h + 1) * dim] = gq[h * tok : (h + 1) * tok]
    stores[1].start()

    for part, out, store in ((1, gv_ref, stores[3]), (0, gk_ref, stores[2])):
        total = g_mine[part]
        for d in range(1, group):
            grad_copies[part, d].wait_recv()
            total = total + g_recv[part, d].astype(F32)
        out[...] = total.T.astype(BF16)
        store.start()

    for copy in list(kv_copies.values()) + kv_forwards:
        copy.wait_send()
    for copy in list(prev_copies.values()) + list(grad_copies.values()):
        copy.wait_send()
    for store in stores:
        store.wait()


def store_kernel(*refs):
    count = (len(refs) - 1) // 2
    sems = refs[-1]
    copies = [
        pltpu.make_async_copy(refs[n], refs[count + n], sems.at[n]) for n in range(count)
    ]
    for copy in copies:
        copy.start()
    for copy in copies:
        copy.wait()


def solution(mesh):
    segments, group = mesh.shape["outer"], mesh.shape["inner"]

    def body(queries, key_vectors, value_vectors, grad_output, positions):
        tok, full = queries.shape
        dim = key_vectors.shape[1]
        heads = full // dim
        blocks, rows = 2 * group, heads * tok
        keys = blocks * tok
        scratch = [
            ((tok, full), BF16),
            ((tok, full), BF16),
            ((1, tok), jnp.int32),
            ((group, 2 * tok + 16, dim), BF16),
            ((group, 2 * tok, dim), BF16),
            ((rows, dim), BF16),
            ((rows, dim), BF16),
            ((dim, rows), BF16),
            ((dim, rows), BF16),
            ((rows, keys), F32),
            ((rows, keys), F32),
            ((rows, keys), BF16),
            ((2, group, dim, tok), BF16),
            ((2, group, dim, tok), BF16),
            ((2, group, dim, tok), BF16),
            ((2, group, dim, tok), BF16),
            ((2, dim, tok), F32),
            ((tok, full), BF16),
            ((tok, full), BF16),
            ((tok, dim), BF16),
            ((tok, dim), BF16),
        ]
        hbm = pl.BlockSpec(memory_space=pl.ANY)
        results = [
            jax.ShapeDtypeStruct(queries.shape, BF16),
            jax.ShapeDtypeStruct(queries.shape, BF16),
            jax.ShapeDtypeStruct(key_vectors.shape, BF16),
            jax.ShapeDtypeStruct(key_vectors.shape, BF16),
        ]
        sem = pltpu.SemaphoreType.DMA
        made = pl.pallas_call(
            functools.partial(kernel, segments, group, heads, dim, tok),
            out_shape=results,
            in_specs=[hbm] * 5,
            out_specs=[hbm] * 4,
            scratch_shapes=[pltpu.VMEM(s, t) for s, t in scratch]
            + [sem((5,)), sem((4,))]
            + [sem((group,))] * 4
            + [sem((2, group))] * 4,
            compiler_params=pltpu.CompilerParams(
                collective_id=0, has_side_effects=True, vmem_limit_bytes=vmem_bytes
            ),
            name="window_attention",
        )(queries, key_vectors, value_vectors, grad_output, positions.reshape(1, tok))
        return pl.pallas_call(
            store_kernel,
            out_shape=results,
            in_specs=[hbm] * 4,
            out_specs=[hbm] * 4,
            scratch_shapes=[sem((4,))],
            name="store_results",
        )(*made)

    rows = P(("outer", "inner"), None)
    return jax.shard_map(
        body,
        mesh=mesh,
        in_specs=(rows, rows, rows, rows, P(("outer", "inner"))),
        out_specs=(rows, rows, rows, rows),
        check_vma=False,
    )
```

time: 41 us -> 47 us (1.15)
  the two profiles are of different devices: /device:TPU:0 before, /device:TPU:1 now
where the time goes in v2:
time: 47 us; the launch traced here: 46.5 us
  Pallas kernels  45.8 us (97%)
  between operations  0.64 us (1%)
    pallas_call x1, Pallas kernels, body(): pl.pallas_call(functools.partial(kernel, segments, group, heads, dim, tok...  26.8 us
    pallas_call x1, Pallas kernels, body(): pl.pallas_call(store_kernel, out_shape=results, in_specs=[hbm] * 4, out_s...  19 us

profile of v2, /device:TPU:1, one launch (start us, length us, event | category | flops | bytes accessed | tf_op | source)
XLA Modules:
  0.0 46.5 jit_solution(1158864181850267029)
XLA Ops:
  0.6 26.8 %window_attention.1 = (bf16[128,1024]{1,0:T(8,128)(2,1)}, bf16[128,1024]{1,0:T(8,128)(2,1)}, bf16[128,128]{1,0:T(8,128)(2,1)}, bf16[128,128]{1,0:T(8,128)(2,1)}) custom-call(bf16[128,1024]{1,0:T(8,128)(2,1)} %q_hbm.1, bf16[128,128]{1,0:T(8,128)(2,1)} %k_hbm.1, bf16[128,128]{1,0:T(8,128)(2,1)} %v_hbm.1, bf16[128,1024]{1,0:T(8,128)(2,1)} %do_hbm.1, ...), custom_call_target="tpu_custom_call" | custom-call | tf_op jit(solution)/shard_map/window_attention/pallas_call | solution.py:288
  27.5 19.0 %store_results.1 = (bf16[128,1024]{1,0:T(8,128)(2,1)}, bf16[128,1024]{1,0:T(8,128)(2,1)}, bf16[128,128]{1,0:T(8,128)(2,1)}, bf16[128,128]{1,0:T(8,128)(2,1)}) custom-call(bf16[128,1024]{1,0:T(8,128)(2,1)} %get-tuple-element.8.refs_0_, bf16[128,1024]{1,0:T(8,128)(2,1)} %get-tuple-element.9.refs_1_, bf16[128,128]{1,0:T(8,128)(2,1)} %get-tuple-element.10.refs_2_, ...), custom_call_target="tpu_custom_call" | custom-call | tf_op jit(solution)/shard_map/store_results/pallas_call | solution.py:302

commit v3 on v2

v3 whole, which is shorter than its diff:
```python
import functools
import math

import jax
import jax.numpy as jnp
from jax import lax
from jax.experimental import pallas as pl
from jax.experimental.pallas import tpu as pltpu
from jax.sharding import PartitionSpec as P

masked_score = -1e30
vmem_bytes = (64 << 20) - (600 << 10)
MESH = pl.DeviceIdType.MESH
F32 = jnp.float32
BF16 = jnp.bfloat16


def dot_nt(a, b):
    return lax.dot_general(a, b, (((1,), (1,)), ((), ())), preferred_element_type=F32)


def dot_nn(a, b):
    return lax.dot_general(a, b, (((1,), (0,)), ((), ())), preferred_element_type=F32)


def kernel(
    segments, group, heads, dim, tok,
    q_hbm, k_hbm, v_hbm, do_hbm, pos_hbm,
    att_hbm, gq_hbm, mine_hbm, recv_hbm,
    q_ref, do_ref, pos_ref, k_own, v_own, k_prev, v_prev, qs, dos, q_t, do_t, s_ref, dp_ref, w_ref,
    p_send, p_recv, g_send, g_mine, att_ref, gq_ref,
    in_sem, out_sem, k_ssem, k_rsem, v_ssem, v_rsem, kf_ssem, kf_rsem, vf_ssem, vf_rsem,
    p_ssem, p_rsem, g_ssem, g_rsem,
):
    seg = lax.axis_index("outer")
    me = lax.axis_index("inner")
    nxt = lax.rem(seg + 1, segments)
    prv = lax.rem(seg + segments - 1, segments)
    scale = float(dim) ** -0.5
    blocks = 2 * group

    loads = [
        pltpu.make_async_copy(k_hbm, k_own.at[0, pl.ds(0, tok)], in_sem.at[0]),
        pltpu.make_async_copy(pos_hbm, pos_ref, in_sem.at[1]),
        pltpu.make_async_copy(v_hbm, v_own.at[0], in_sem.at[2]),
        pltpu.make_async_copy(q_hbm, q_ref, in_sem.at[3]),
        pltpu.make_async_copy(do_hbm, do_ref, in_sem.at[4]),
    ]
    stores = [
        pltpu.make_async_copy(att_ref, att_hbm, out_sem.at[0]),
        pltpu.make_async_copy(gq_ref, gq_hbm, out_sem.at[1]),
        pltpu.make_async_copy(g_mine.at[0], mine_hbm.at[0], out_sem.at[2]),
        pltpu.make_async_copy(g_mine.at[1], mine_hbm.at[1], out_sem.at[3]),
    ]
    for load in loads:
        load.start()

    barrier = pltpu.get_barrier_semaphore()
    partners = [(seg, lax.rem(me + d, group)) for d in range(1, group)] + [(nxt, me), (prv, me)]
    for partner in partners:
        pl.semaphore_signal(barrier, inc=1, device_id=partner, device_id_type=MESH)

    for load in loads[:3]:
        load.wait()
    pos = pos_ref[...]
    pos_hi = jnp.broadcast_to((pos >> 7).astype(F32), (8, tok))
    pos_lo = jnp.broadcast_to((pos & 127).astype(F32), (8, tok))
    k_own[0, tok:, :] = jnp.concatenate([pos_hi, pos_lo], axis=0).astype(BF16)
    pl.semaphore_wait(barrier, len(partners))

    def gather(buf, ssem, rsem, d):
        return pltpu.make_async_remote_copy(
            src_ref=buf.at[0], dst_ref=buf.at[d], send_sem=ssem.at[d], recv_sem=rsem.at[d],
            device_id=(seg, lax.rem(me + group - d, group)), device_id_type=MESH,
        )

    def forward(src, dst, ssem, rsem, d):
        return pltpu.make_async_remote_copy(
            src_ref=src.at[d, pl.ds(0, tok)], dst_ref=dst.at[d],
            send_sem=ssem.at[d], recv_sem=rsem.at[d],
            device_id=(nxt, me), device_id_type=MESH,
        )

    others = range(1, group)
    k_copies = {d: gather(k_own, k_ssem, k_rsem, d) for d in others}
    v_copies = {d: gather(v_own, v_ssem, v_rsem, d) for d in others}
    k_forwards = [forward(k_own, k_prev, kf_ssem, kf_rsem, d) for d in range(group)]
    v_forwards = [forward(v_own, v_prev, vf_ssem, vf_rsem, d) for d in range(group)]
    for d in others:
        k_copies[d].start()
    k_forwards[0].start()

    for load in loads[3:]:
        load.wait()
    for h in range(heads):
        rows, cols = slice(h * tok, (h + 1) * tok), slice(h * dim, (h + 1) * dim)
        q_h, do_h = q_ref[:, cols], do_ref[:, cols]
        qs[rows, :] = q_h
        dos[rows, :] = do_h
        q_t[:, rows] = q_h.astype(F32).T.astype(BF16)
        do_t[:, rows] = do_h.astype(F32).T.astype(BF16)
    for d in others:
        v_copies[d].start()
    v_forwards[0].start()

    pos_col = jnp.broadcast_to(pos.astype(F32), (tok, tok)).T
    prev_bias = jnp.where(seg > 0, 0.0, masked_score).astype(F32)

    def keys_of(block):
        return k_own[block, 0:tok, :] if block < group else k_prev[block - group]

    def values_of(block):
        return v_own[block] if block < group else v_prev[block - group]

    def bias_of(block):
        if block >= group:
            return jnp.broadcast_to(prev_bias, (tok, tok))
        coded = k_own[block, tok:, :].astype(F32)
        key_pos = coded[0:1, :] * 128.0 + coded[8:9, :]
        return jnp.where(key_pos <= pos_col, 0.0, masked_score)

    def cat(parts, axis):
        return parts[0] if len(parts) == 1 else jnp.concatenate(parts, axis=axis)

    def columns(step):
        return slice(step[0] * tok, (step[-1] + 1) * tok)

    def score_step(step):
        width = len(step) * tok
        score = dot_nt(qs[...], cat([keys_of(b) for b in step], 0))
        bias = cat([bias_of(b) for b in step], 1)
        score = score.reshape(heads, tok, width) + bias[None]
        s_ref[:, columns(step)] = score.reshape(heads * tok, width)

    def grad_step(step):
        dp_ref[:, columns(step)] = dot_nt(dos[...], cat([values_of(b) for b in step], 0))

    score_step([0])
    for d in others:
        k_copies[d].wait_recv()
        k_forwards[d].start()
        if d == 1:
            score_step([1])
        elif d % 2 == 1:
            score_step([d - 1, d])

    rate = scale * math.log2(math.e)
    own, prev = slice(0, group * tok), slice(group * tok, blocks * tok)
    own_top, own_sum = [], []
    for h in range(heads):
        rows = slice(h * tok, (h + 1) * tok)
        s = s_ref[rows, own]
        top = jnp.max(s, axis=1, keepdims=True)
        e = jnp.exp2((s - top) * rate)
        s_ref[rows, own] = e
        own_top.append(top)
        own_sum.append(jnp.sum(e, axis=1, keepdims=True))

    for d in others:
        v_copies[d].wait_recv()
        v_forwards[d].start()
    for d in range(0, group, 2):
        grad_step([d, d + 1])

    for d in range(0, group, 2):
        k_forwards[d].wait_recv()
        k_forwards[d + 1].wait_recv()
        score_step([group + d, group + d + 1])
    for h in range(heads):
        rows = slice(h * tok, (h + 1) * tok)
        s = s_ref[rows, prev]
        top = jnp.maximum(own_top[h], jnp.max(s, axis=1, keepdims=True))
        e = jnp.exp2((s - top) * rate)
        shrink = jnp.exp2((own_top[h] - top) * rate)
        inv = 1.0 / (own_sum[h] * shrink + jnp.sum(e, axis=1, keepdims=True))
        w_ref[rows, prev] = (e * inv).astype(BF16)
        w_ref[rows, own] = (s_ref[rows, own] * (shrink * inv)).astype(BF16)

    def prev_copy(part, first):
        return pltpu.make_async_remote_copy(
            src_ref=p_send.at[part, pl.ds(first, 2)], dst_ref=p_recv.at[part, pl.ds(first, 2)],
            send_sem=p_ssem.at[part, first], recv_sem=p_rsem.at[part, first],
            device_id=(prv, me), device_id_type=MESH,
        )

    def grad_copy(part, d):
        return pltpu.make_async_remote_copy(
            src_ref=g_send.at[part, d], dst_ref=recv_hbm.at[part, d - 1],
            send_sem=g_ssem.at[part, d], recv_sem=g_rsem.at[part, d],
            device_id=(seg, lax.rem(me + d, group)), device_id_type=MESH,
        )

    firsts = list(range(0, group, 2))
    prev_copies = {(p, f): prev_copy(p, f) for p in range(2) for f in firsts}
    grad_copies = {(p, d): grad_copy(p, d) for p in range(2) for d in others}

    def pair(first):
        return columns([first, first + 1])

    def send_prev(part, first, total):
        for n in range(2):
            p_send[part, first + n] = total[:, n * tok : (n + 1) * tok].astype(BF16)
        prev_copies[part, first].start()

    def send_own(part, first, total):
        prev_copies[part, first].wait_recv()
        for n in (1, 0):
            d = first + n
            block = total[:, n * tok : (n + 1) * tok] + p_recv[part, d].astype(F32)
            if d == 0:
                g_mine[part] = block
                stores[2 + part].start()
            else:
                g_send[part, d] = block.astype(BF16)
                grad_copies[part, d].start()

    def key_terms(first):
        cols = pair(first)
        ds = (w_ref[:, cols].astype(F32) * (dp_ref[:, cols] - delta)).astype(BF16)
        w_ref[:, cols] = ds
        return dot_nn(q_t[...], ds) * scale

    for first in firsts:
        send_prev(1, first, dot_nn(do_t[...], w_ref[:, pair(group + first)]))

    for d in range(0, group, 2):
        v_forwards[d].wait_recv()
        v_forwards[d + 1].wait_recv()
        grad_step([group + d, group + d + 1])
    all_values = cat([values_of(b) for b in range(blocks)], 0)
    attended = dot_nn(w_ref[...], all_values).astype(BF16)
    delta = jnp.sum(dos[...].astype(F32) * attended.astype(F32), axis=1, keepdims=True)
    for h in range(heads):
        att_ref[:, h * dim : (h + 1) * dim] = attended[h * tok : (h + 1) * tok]
    stores[0].start()

    for first in firsts[::-1]:
        send_own(1, first, dot_nn(do_t[...], w_ref[:, pair(first)]))
    for first in firsts:
        send_prev(0, first, key_terms(group + first))
    for first in firsts[::-1]:
        send_own(0, first, key_terms(first))

    all_keys = cat([keys_of(b) for b in range(blocks)], 0)
    gq = (dot_nn(w_ref[...], all_keys) * scale).astype(BF16)
    for h in range(heads):
        gq_ref[:, h * dim : (h + 1) * dim] = gq[h * tok : (h + 1) * tok]
    stores[1].start()

    for copy in list(k_copies.values()) + list(v_copies.values()) + k_forwards + v_forwards:
        copy.wait_send()
    for copy in list(prev_copies.values()) + list(grad_copies.values()):
        copy.wait_send()
    for store in stores:
        store.wait()
    for copy in grad_copies.values():
        copy.wait_recv()


def store_kernel(
    group,
    att_hbm, gq_hbm, mine_hbm, recv_hbm, att_out, gq_out, gk_out, gv_out,
    att_ref, gq_ref, mine_ref, recv_ref, gk_ref, gv_ref, in_sem, out_sem,
):
    moves = ((mine_hbm, mine_ref), (recv_hbm, recv_ref), (att_hbm, att_ref), (gq_hbm, gq_ref))
    loads = [pltpu.make_async_copy(a, b, in_sem.at[n]) for n, (a, b) in enumerate(moves)]
    moves = ((att_ref, att_out), (gq_ref, gq_out), (gk_ref, gk_out), (gv_ref, gv_out))
    stores = [pltpu.make_async_copy(a, b, out_sem.at[n]) for n, (a, b) in enumerate(moves)]
    for load in loads:
        load.start()
    loads[0].wait()
    loads[1].wait()
    for part, out in ((0, gk_ref), (1, gv_ref)):
        total = mine_ref[part]
        for d in range(group - 1):
            total = total + recv_ref[part, d].astype(F32)
        out[...] = total.T.astype(BF16)
        stores[2 + part].start()
    for n in range(2):
        loads[2 + n].wait()
        stores[n].start()
    for store in stores:
        store.wait()


def solution(mesh):
    segments, group = mesh.shape["outer"], mesh.shape["inner"]

    def body(queries, key_vectors, value_vectors, grad_output, positions):
        tok, full = queries.shape
        dim = key_vectors.shape[1]
        heads = full // dim
        blocks, rows = 2 * group, heads * tok
        keys = blocks * tok
        wide, narrow = (tok, full), (tok, dim)
        scratch = [
            (wide, BF16),
            (wide, BF16),
            ((1, tok), jnp.int32),
            ((group, tok + 16, dim), BF16),
            ((group, tok, dim), BF16),
            ((group, tok, dim), BF16),
            ((group, tok, dim), BF16),
            ((rows, dim), BF16),
            ((rows, dim), BF16),
            ((dim, rows), BF16),
            ((dim, rows), BF16),
            ((rows, keys), F32),
            ((rows, keys), F32),
            ((rows, keys), BF16),
            ((2, group, dim, tok), BF16),
            ((2, group, dim, tok), BF16),
            ((2, group, dim, tok), BF16),
            ((2, dim, tok), F32),
            (wide, BF16),
            (wide, BF16),
        ]
        made = [(wide, BF16), (wide, BF16), ((2, dim, tok), F32), ((2, group - 1, dim, tok), BF16)]
        results = [(wide, BF16), (wide, BF16), (narrow, BF16), (narrow, BF16)]
        hbm = pl.BlockSpec(memory_space=pl.ANY)
        sem = pltpu.SemaphoreType.DMA
        partial = pl.pallas_call(
            functools.partial(kernel, segments, group, heads, dim, tok),
            out_shape=[jax.ShapeDtypeStruct(s, t) for s, t in made],
            in_specs=[hbm] * 5,
            out_specs=[hbm] * 4,
            scratch_shapes=[pltpu.VMEM(s, t) for s, t in scratch]
            + [sem((5,)), sem((4,))]
            + [sem((group,))] * 8
            + [sem((2, group))] * 4,
            compiler_params=pltpu.CompilerParams(
                collective_id=0, has_side_effects=True, vmem_limit_bytes=vmem_bytes
            ),
            name="window_attention",
        )(queries, key_vectors, value_vectors, grad_output, positions.reshape(1, tok))
        return pl.pallas_call(
            functools.partial(store_kernel, group),
            out_shape=[jax.ShapeDtypeStruct(s, t) for s, t in results],
            in_specs=[hbm] * 4,
            out_specs=[hbm] * 4,
            scratch_shapes=[pltpu.VMEM(s, t) for s, t in made + results[2:]] + [sem((4,))] * 2,
            compiler_params=pltpu.CompilerParams(vmem_limit_bytes=vmem_bytes),
            name="store_results",
        )(*partial)

    rows = P(("outer", "inner"), None)
    return jax.shard_map(
        body,
        mesh=mesh,
        in_specs=(rows, rows, rows, rows, P(("outer", "inner"))),
        out_specs=(rows, rows, rows, rows),
        check_vma=False,
    )
```

time: 47 us -> 29.1 us (0.62)
  Pallas kernels: 45.8 us -> 28 us
    pallas_call x1, Pallas kernels: 19 us -> 1.98 us  [body(): pl.pallas_call(functools.partial(store_kernel, group), out_shape=[jax.Sha...]
    pallas_call x1, Pallas kernels: 26.8 us -> 26.1 us  [body(): pl.pallas_call(functools.partial(kernel, segments, group, heads, dim, tok...]
where the time goes in v3:
time: 29.1 us; the launch traced here: 28.7 us
  Pallas kernels  28 us (96%)
  between operations  0.64 us (2%)
    pallas_call x1, Pallas kernels, body(): pl.pallas_call(functools.partial(kernel, segments, group, heads, dim, tok...  26.1 us
    pallas_call x1, Pallas kernels, body(): pl.pallas_call(functools.partial(store_kernel, group), out_shape=[jax.Sha...  1.98 us

profile of v3, /device:TPU:1, one launch (start us, length us, event | category | flops | bytes accessed | tf_op | source)
XLA Modules:
  0.0 28.7 jit_solution(12716138558686482941)
XLA Ops:
  0.6 26.1 %window_attention.1 = (bf16[128,1024]{1,0:T(8,128)(2,1)}, bf16[128,1024]{1,0:T(8,128)(2,1)}, f32[2,128,128]{2,1,0:T(8,128)}, bf16[2,3,128,128]{3,2,1,0:T(8,128)(2,1)}) custom-call(bf16[128,1024]{1,0:T(8,128)(2,1)} %q_hbm.1, bf16[128,128]{1,0:T(8,128)(2,1)} %k_hbm.1, bf16[128,128]{1,0:T(8,128)(2,1)} %v_hbm.1, bf16[128,1024]{1,0:T(8,128)(2,1)} %do_hbm.1, ...), custom_call_target="tpu_custom_call" | custom-call | tf_op jit(solution)/shard_map/window_attention/pallas_call | solution.py:322
  26.7 2.0 %store_results.1 = (bf16[128,1024]{1,0:T(8,128)(2,1)}, bf16[128,1024]{1,0:T(8,128)(2,1)}, bf16[128,128]{1,0:T(8,128)(2,1)}, bf16[128,128]{1,0:T(8,128)(2,1)}) custom-call(bf16[128,1024]{1,0:T(8,128)(2,1)} %get-tuple-element.8.att_hbm, bf16[128,1024]{1,0:T(8,128)(2,1)} %get-tuple-element.9.gq_hbm, f32[2,128,128]{2,1,0:T(8,128)} %get-tuple-element.10.mine_hbm, ...), custom_call_target="tpu_custom_call" | custom-call | tf_op jit(solution)/shard_map/store_results/pallas_call | solution.py:336

commit v4 on v3

--- a/solution.py
+++ b/solution.py
@@ -28,7 +28,7 @@
     q_hbm, k_hbm, v_hbm, do_hbm, pos_hbm,
     att_hbm, gq_hbm, mine_hbm, recv_hbm,
     q_ref, do_ref, pos_ref, k_own, v_own, k_prev, v_prev, qs, dos, q_t, do_t, s_ref, dp_ref, w_ref,
-    p_send, p_recv, g_send, g_mine, att_ref, gq_ref,
+    p_send, p_recv, g_send, g_mine, att_ref, gq_ref, pos_col, top_ref, sum_ref, delta_ref,
     in_sem, out_sem, k_ssem, k_rsem, v_ssem, v_rsem, kf_ssem, kf_rsem, vf_ssem, vf_rsem,
     p_ssem, p_rsem, g_ssem, g_rsem,
 ):
@@ -92,94 +92,83 @@
 
     for load in loads[3:]:
         load.wait()
-    for h in range(heads):
-        rows, cols = slice(h * tok, (h + 1) * tok), slice(h * dim, (h + 1) * dim)
+
+    @pl.loop(0, heads)
+    def _(h):
+        rows, cols = pl.ds(h * tok, tok), pl.ds(h * dim, dim)
         q_h, do_h = q_ref[:, cols], do_ref[:, cols]
         qs[rows, :] = q_h
         dos[rows, :] = do_h
         q_t[:, rows] = q_h.astype(F32).T.astype(BF16)
         do_t[:, rows] = do_h.astype(F32).T.astype(BF16)
+
     for d in others:
         v_copies[d].start()
     v_forwards[0].start()
 
-    pos_col = jnp.broadcast_to(pos.astype(F32), (tok, tok)).T
+    pos_col[...] = jnp.broadcast_to(pos.astype(F32), (tok, tok)).T
     prev_bias = jnp.where(seg > 0, 0.0, masked_score).astype(F32)
-
-    def keys_of(block):
-        return k_own[block, 0:tok, :] if block < group else k_prev[block - group]
-
-    def values_of(block):
-        return v_own[block] if block < group else v_prev[block - group]
-
-    def bias_of(block):
-        if block >= group:
-            return jnp.broadcast_to(prev_bias, (tok, tok))
-        coded = k_own[block, tok:, :].astype(F32)
+    own, prev = slice(0, group * tok), slice(group * tok, blocks * tok)
+    pairs, span = group // 2, 2 * tok
+
+    @pl.loop(0, group)
+    def _(d):
+        @pl.when(d > 0)
+        def _():
+            gather(k_own, k_ssem, k_rsem, d).wait_recv()
+            forward(k_own, k_prev, kf_ssem, kf_rsem, d).start()
+
+        coded = k_own[d, tok:, :].astype(F32)
         key_pos = coded[0:1, :] * 128.0 + coded[8:9, :]
-        return jnp.where(key_pos <= pos_col, 0.0, masked_score)
-
-    def cat(parts, axis):
-        return parts[0] if len(parts) == 1 else jnp.concatenate(parts, axis=axis)
-
-    def columns(step):
-        return slice(step[0] * tok, (step[-1] + 1) * tok)
-
-    def score_step(step):
-        width = len(step) * tok
-        score = dot_nt(qs[...], cat([keys_of(b) for b in step], 0))
-        bias = cat([bias_of(b) for b in step], 1)
-        score = score.reshape(heads, tok, width) + bias[None]
-        s_ref[:, columns(step)] = score.reshape(heads * tok, width)
-
-    def grad_step(step):
-        dp_ref[:, columns(step)] = dot_nt(dos[...], cat([values_of(b) for b in step], 0))
-
-    score_step([0])
-    for d in others:
-        k_copies[d].wait_recv()
-        k_forwards[d].start()
-        if d == 1:
-            score_step([1])
-        elif d % 2 == 1:
-            score_step([d - 1, d])
+        bias = jnp.where(key_pos <= pos_col[...], 0.0, masked_score)
+        score = dot_nt(qs[...], k_own[d, 0:tok, :]).reshape(heads, tok, tok) + bias[None]
+        s_ref[:, pl.ds(d * tok, tok)] = score.reshape(heads * tok, tok)
 
     rate = scale * math.log2(math.e)
-    own, prev = slice(0, group * tok), slice(group * tok, blocks * tok)
-    own_top, own_sum = [], []
-    for h in range(heads):
-        rows = slice(h * tok, (h + 1) * tok)
+
+    @pl.loop(0, heads)
+    def _(h):
+        rows = pl.ds(h * tok, tok)
         s = s_ref[rows, own]
         top = jnp.max(s, axis=1, keepdims=True)
         e = jnp.exp2((s - top) * rate)
         s_ref[rows, own] = e
-        own_top.append(top)
-        own_sum.append(jnp.sum(e, axis=1, keepdims=True))
+        top_ref[rows, :] = top
+        sum_ref[rows, :] = jnp.sum(e, axis=1, keepdims=True)
 
     for d in others:
         v_copies[d].wait_recv()
         v_forwards[d].start()
-    for d in range(0, group, 2):
-        grad_step([d, d + 1])
-
-    for d in range(0, group, 2):
-        k_forwards[d].wait_recv()
-        k_forwards[d + 1].wait_recv()
-        score_step([group + d, group + d + 1])
-    for h in range(heads):
-        rows = slice(h * tok, (h + 1) * tok)
+
+    @pl.loop(0, pairs)
+    def _(p):
+        values = v_own[pl.ds(2 * p, 2)].reshape(span, dim)
+        dp_ref[:, pl.ds(p * span, span)] = dot_nt(dos[...], values)
+
+    @pl.loop(0, pairs)
+    def _(p):
+        for n in range(2):
+            forward(k_own, k_prev, kf_ssem, kf_rsem, 2 * p + n).wait_recv()
+        score = dot_nt(qs[...], k_prev[pl.ds(2 * p, 2)].reshape(span, dim))
+        s_ref[:, pl.ds((pairs + p) * span, span)] = score + prev_bias
+
+    @pl.loop(0, heads)
+    def _(h):
+        rows = pl.ds(h * tok, tok)
         s = s_ref[rows, prev]
-        top = jnp.maximum(own_top[h], jnp.max(s, axis=1, keepdims=True))
+        own_top = top_ref[rows, :]
+        top = jnp.maximum(own_top, jnp.max(s, axis=1, keepdims=True))
         e = jnp.exp2((s - top) * rate)
-        shrink = jnp.exp2((own_top[h] - top) * rate)
-        inv = 1.0 / (own_sum[h] * shrink + jnp.sum(e, axis=1, keepdims=True))
+        shrink = jnp.exp2((own_top - top) * rate)
+        inv = 1.0 / (sum_ref[rows, :] * shrink + jnp.sum(e, axis=1, keepdims=True))
         w_ref[rows, prev] = (e * inv).astype(BF16)
         w_ref[rows, own] = (s_ref[rows, own] * (shrink * inv)).astype(BF16)
 
-    def prev_copy(part, first):
+    def prev_copy(part, p):
+        two = pl.ds(2 * p, 2)
         return pltpu.make_async_remote_copy(
-            src_ref=p_send.at[part, pl.ds(first, 2)], dst_ref=p_recv.at[part, pl.ds(first, 2)],
-            send_sem=p_ssem.at[part, first], recv_sem=p_rsem.at[part, first],
+            src_ref=p_send.at[part, two], dst_ref=p_recv.at[part, two],
+            send_sem=p_ssem.at[part, p], recv_sem=p_rsem.at[part, p],
             device_id=(prv, me), device_id_type=MESH,
         )
 
@@ -190,70 +179,90 @@
             device_id=(seg, lax.rem(me + d, group)), device_id_type=MESH,
         )
 
-    firsts = list(range(0, group, 2))
-    prev_copies = {(p, f): prev_copy(p, f) for p in range(2) for f in firsts}
-    grad_copies = {(p, d): grad_copy(p, d) for p in range(2) for d in others}
-
-    def pair(first):
-        return columns([first, first + 1])
-
-    def send_prev(part, first, total):
-        for n in range(2):
-            p_send[part, first + n] = total[:, n * tok : (n + 1) * tok].astype(BF16)
-        prev_copies[part, first].start()
-
-    def send_own(part, first, total):
-        prev_copies[part, first].wait_recv()
-        for n in (1, 0):
-            d = first + n
-            block = total[:, n * tok : (n + 1) * tok] + p_recv[part, d].astype(F32)
-            if d == 0:
-                g_mine[part] = block
-                stores[2 + part].start()
-            else:
-                g_send[part, d] = block.astype(BF16)
-                grad_copies[part, d].start()
-
-    def key_terms(first):
-        cols = pair(first)
-        ds = (w_ref[:, cols].astype(F32) * (dp_ref[:, cols] - delta)).astype(BF16)
+    def terms(part, p):
+        cols = pl.ds(p * span, span)
+        if part == 1:
+            return dot_nn(do_t[...], w_ref[:, cols])
+        ds = (w_ref[:, cols].astype(F32) * (dp_ref[:, cols] - delta_ref[...])).astype(BF16)
         w_ref[:, cols] = ds
         return dot_nn(q_t[...], ds) * scale
 
-    for first in firsts:
-        send_prev(1, first, dot_nn(do_t[...], w_ref[:, pair(group + first)]))
-
-    for d in range(0, group, 2):
-        v_forwards[d].wait_recv()
-        v_forwards[d + 1].wait_recv()
-        grad_step([group + d, group + d + 1])
-    all_values = cat([values_of(b) for b in range(blocks)], 0)
-    attended = dot_nn(w_ref[...], all_values).astype(BF16)
-    delta = jnp.sum(dos[...].astype(F32) * attended.astype(F32), axis=1, keepdims=True)
-    for h in range(heads):
-        att_ref[:, h * dim : (h + 1) * dim] = attended[h * tok : (h + 1) * tok]
+    def prev_terms(part):
+        @pl.loop(0, pairs)
+        def _(p):
+            total = terms(part, pairs + p)
+            for n in range(2):
+                p_send[part, 2 * p + n] = total[:, n * tok : (n + 1) * tok].astype(BF16)
+            prev_copy(part, p).start()
+
+    def own_terms(part):
+        @pl.loop(0, pairs)
+        def _(step):
+            p = pairs - 1 - step
+            total = terms(part, p)
+            prev_copy(part, p).wait_recv()
+
+            def send(n):
+                d = 2 * p + n
+                block = total[:, n * tok : (n + 1) * tok] + p_recv[part, d].astype(F32)
+                g_send[part, d] = block.astype(BF16)
+                grad_copy(part, d).start()
+
+            send(1)
+
+            @pl.when(p > 0)
+            def _():
+                send(0)
+
+            @pl.when(p == 0)
+            def _():
+                g_mine[part] = total[:, 0:tok] + p_recv[part, 0].astype(F32)
+                stores[2 + part].start()
+
+    prev_terms(1)
+
+    @pl.loop(0, pairs)
+    def _(p):
+        for n in range(2):
+            forward(v_own, v_prev, vf_ssem, vf_rsem, 2 * p + n).wait_recv()
+        values = v_prev[pl.ds(2 * p, 2)].reshape(span, dim)
+        dp_ref[:, pl.ds((pairs + p) * span, span)] = dot_nt(dos[...], values)
+
+    def weighted(rows, own_part, prev_part):
+        own_part = own_part.reshape(group * tok, dim)
+        prev_part = prev_part.reshape(group * tok, dim)
+        return dot_nn(w_ref[rows, own], own_part) + dot_nn(w_ref[rows, prev], prev_part)
+
+    @pl.loop(0, heads // 2)
+    def _(c):
+        rows = pl.ds(c * span, span)
+        attended = weighted(rows, v_own[...], v_prev[...]).astype(BF16)
+        product = dos[rows, :].astype(F32) * attended.astype(F32)
+        delta_ref[rows, :] = jnp.sum(product, axis=1, keepdims=True)
+        for n in range(2):
+            att_ref[:, pl.ds((2 * c + n) * dim, dim)] = attended[n * tok : (n + 1) * tok]
+
     stores[0].start()
-
-    for first in firsts[::-1]:
-        send_own(1, first, dot_nn(do_t[...], w_ref[:, pair(first)]))
-    for first in firsts:
-        send_prev(0, first, key_terms(group + first))
-    for first in firsts[::-1]:
-        send_own(0, first, key_terms(first))
-
-    all_keys = cat([keys_of(b) for b in range(blocks)], 0)
-    gq = (dot_nn(w_ref[...], all_keys) * scale).astype(BF16)
-    for h in range(heads):
-        gq_ref[:, h * dim : (h + 1) * dim] = gq[h * tok : (h + 1) * tok]
+    own_terms(1)
+    prev_terms(0)
+    own_terms(0)
+
+    @pl.loop(0, heads // 2)
+    def _(c):
+        rows = pl.ds(c * span, span)
+        gq = (weighted(rows, k_own[:, 0:tok, :], k_prev[...]) * scale).astype(BF16)
+        for n in range(2):
+            gq_ref[:, pl.ds((2 * c + n) * dim, dim)] = gq[n * tok : (n + 1) * tok]
+
     stores[1].start()
-
-    for copy in list(k_copies.values()) + list(v_copies.values()) + k_forwards + v_forwards:
-        copy.wait_send()
-    for copy in list(prev_copies.values()) + list(grad_copies.values()):
+    grads = [grad_copy(part, d) for part in range(2) for d in others]
+    returns = [prev_copy(part, p) for part in range(2) for p in range(pairs)]
+    sent = list(k_copies.values()) + list(v_copies.values()) + k_forwards + v_forwards
+    for copy in sent + returns + grads:
         copy.wait_send()
     for store in stores:
         store.wait()
-    for copy in grad_copies.values():
+    for copy in grads:
         copy.wait_recv()
 
 
@@ -314,6 +323,10 @@
             ((2, dim, tok), F32),
             (wide, BF16),
             (wide, BF16),
+            ((tok, tok), F32),
+            ((rows, 1), F32),
+            ((rows, 1), F32),
+            ((rows, 1), F32),
         ]
         made = [(wide, BF16), (wide, BF16), ((2, dim, tok), F32), ((2, group - 1, dim, tok), BF16)]
         results = [(wide, BF16), (wide, BF16), (narrow, BF16), (narrow, BF16)]

time: 29.1 us -> 33.2 us (1.14)
  Pallas kernels: 28 us -> 32.1 us
    pallas_call x1, Pallas kernels: 26.1 us -> 30.1 us  [body(): pl.pallas_call(functools.partial(kernel, segments, group, heads, dim, tok...]
where the time goes in v4:
time: 33.2 us; the launch traced here: 32.8 us
  Pallas kernels  32.1 us (97%)
  between operations  0.64 us (2%)
    pallas_call x1, Pallas kernels, body(): pl.pallas_call(functools.partial(kernel, segments, group, heads, dim, tok...  30.1 us
    pallas_call x1, Pallas kernels, body(): pl.pallas_call(functools.partial(store_kernel, group), out_shape=[jax.Sha...  1.98 us

profile of v4, /device:TPU:1, one launch (start us, length us, event | category | flops | bytes accessed | tf_op | source)
XLA Modules:
  0.0 32.8 jit_solution(8393317853572487782)
XLA Ops:
  0.6 30.1 %window_attention.1 = (bf16[128,1024]{1,0:T(8,128)(2,1)}, bf16[128,1024]{1,0:T(8,128)(2,1)}, f32[2,128,128]{2,1,0:T(8,128)}, bf16[2,3,128,128]{3,2,1,0:T(8,128)(2,1)}) custom-call(bf16[128,1024]{1,0:T(8,128)(2,1)} %q_hbm.1, bf16[128,128]{1,0:T(8,128)(2,1)} %k_hbm.1, bf16[128,128]{1,0:T(8,128)(2,1)} %v_hbm.1, bf16[128,1024]{1,0:T(8,128)(2,1)} %do_hbm.1, ...), custom_call_target="tpu_custom_call" | custom-call | tf_op jit(solution)/shard_map/window_attention/pallas_call | solution.py:335
  30.8 2.0 %store_results.1 = (bf16[128,1024]{1,0:T(8,128)(2,1)}, bf16[128,1024]{1,0:T(8,128)(2,1)}, bf16[128,128]{1,0:T(8,128)(2,1)}, bf16[128,128]{1,0:T(8,128)(2,1)}) custom-call(bf16[128,1024]{1,0:T(8,128)(2,1)} %get-tuple-element.8.att_hbm, bf16[128,1024]{1,0:T(8,128)(2,1)} %get-tuple-element.9.gq_hbm, f32[2,128,128]{2,1,0:T(8,128)} %get-tuple-element.10.mine_hbm, ...), custom_call_target="tpu_custom_call" | custom-call | tf_op jit(solution)/shard_map/store_results/pallas_call | solution.py:349

commit v5 on v3

--- a/solution.py
+++ b/solution.py
@@ -27,8 +27,8 @@
     segments, group, heads, dim, tok,
     q_hbm, k_hbm, v_hbm, do_hbm, pos_hbm,
     att_hbm, gq_hbm, mine_hbm, recv_hbm,
-    q_ref, do_ref, pos_ref, k_own, v_own, k_prev, v_prev, qs, dos, q_t, do_t, s_ref, dp_ref, w_ref,
-    p_send, p_recv, g_send, g_mine, att_ref, gq_ref,
+    q_ref, do_ref, pos_ref, k_own, v_own, k_prev, v_prev, qs, dos, q_t, do_t, s_ref, dp_ref, w_ref, ds_ref,
+    p_send, p_recv, g_send, g_own, g_mine, att_ref, gq_ref,
     in_sem, out_sem, k_ssem, k_rsem, v_ssem, v_rsem, kf_ssem, kf_rsem, vf_ssem, vf_rsem,
     p_ssem, p_rsem, g_ssem, g_rsem,
 ):
@@ -135,14 +135,21 @@
     def grad_step(step):
         dp_ref[:, columns(step)] = dot_nt(dos[...], cat([values_of(b) for b in step], 0))
 
+    short = jnp.minimum(me, group - 1 - me)
+    ahead = jnp.where(me < group // 2, 1, -1)
+    nearest = []
+    for n in others:
+        both_ways = (n + 1) // 2 * (1 if n % 2 == 1 else -1)
+        offset = jnp.where(n <= 2 * short, both_ways, (n - short) * ahead)
+        nearest.append(lax.rem(offset + group, group))
+
     score_step([0])
-    for d in others:
-        k_copies[d].wait_recv()
-        k_forwards[d].start()
-        if d == 1:
-            score_step([1])
-        elif d % 2 == 1:
-            score_step([d - 1, d])
+    for d in nearest:
+        gather(k_own, k_ssem, k_rsem, d).wait_recv()
+        forward(k_own, k_prev, kf_ssem, kf_rsem, d).start()
+    score_step([1])
+    for d in range(2, group, 2):
+        score_step([d, d + 1])
 
     rate = scale * math.log2(math.e)
     own, prev = slice(0, group * tok), slice(group * tok, blocks * tok)
@@ -156,16 +163,21 @@
         own_top.append(top)
         own_sum.append(jnp.sum(e, axis=1, keepdims=True))
 
-    for d in others:
-        v_copies[d].wait_recv()
-        v_forwards[d].start()
+    for d in nearest:
+        gather(v_own, v_ssem, v_rsem, d).wait_recv()
+        forward(v_own, v_prev, vf_ssem, vf_rsem, d).start()
     for d in range(0, group, 2):
         grad_step([d, d + 1])
+    own_delta = []
+    for h in range(heads):
+        rows = slice(h * tok, (h + 1) * tok)
+        own_delta.append(jnp.sum(s_ref[rows, own] * dp_ref[rows, own], axis=1, keepdims=True))
 
     for d in range(0, group, 2):
         k_forwards[d].wait_recv()
         k_forwards[d + 1].wait_recv()
         score_step([group + d, group + d + 1])
+    own_scale = []
     for h in range(heads):
         rows = slice(h * tok, (h + 1) * tok)
         s = s_ref[rows, prev]
@@ -174,7 +186,7 @@
         shrink = jnp.exp2((own_top[h] - top) * rate)
         inv = 1.0 / (own_sum[h] * shrink + jnp.sum(e, axis=1, keepdims=True))
         w_ref[rows, prev] = (e * inv).astype(BF16)
-        w_ref[rows, own] = (s_ref[rows, own] * (shrink * inv)).astype(BF16)
+        own_scale.append(shrink * inv)
 
     def prev_copy(part, first):
         return pltpu.make_async_remote_copy(
@@ -202,47 +214,61 @@
             p_send[part, first + n] = total[:, n * tok : (n + 1) * tok].astype(BF16)
         prev_copies[part, first].start()
 
-    def send_own(part, first, total):
-        prev_copies[part, first].wait_recv()
-        for n in (1, 0):
-            d = first + n
-            block = total[:, n * tok : (n + 1) * tok] + p_recv[part, d].astype(F32)
-            if d == 0:
-                g_mine[part] = block
-                stores[2 + part].start()
-            else:
-                g_send[part, d] = block.astype(BF16)
-                grad_copies[part, d].start()
+    def send_own(part):
+        for first in firsts[::-1]:
+            prev_copies[part, first].wait_recv()
+            for d in (first + 1, first):
+                block = g_own[part, d] + p_recv[part, d].astype(F32)
+                if d == 0:
+                    g_mine[part] = block
+                    stores[2 + part].start()
+                else:
+                    g_send[part, d] = block.astype(BF16)
+                    grad_copies[part, d].start()
+
+    def keep_own(part, first, total):
+        for n in range(2):
+            g_own[part, first + n] = total[:, n * tok : (n + 1) * tok]
 
     def key_terms(first):
         cols = pair(first)
         ds = (w_ref[:, cols].astype(F32) * (dp_ref[:, cols] - delta)).astype(BF16)
-        w_ref[:, cols] = ds
+        ds_ref[:, cols] = ds
         return dot_nn(q_t[...], ds) * scale
 
     for first in firsts:
         send_prev(1, first, dot_nn(do_t[...], w_ref[:, pair(group + first)]))
 
+    for h in range(heads):
+        rows = slice(h * tok, (h + 1) * tok)
+        w_ref[rows, own] = (s_ref[rows, own] * own_scale[h]).astype(BF16)
     for d in range(0, group, 2):
         v_forwards[d].wait_recv()
         v_forwards[d + 1].wait_recv()
         grad_step([group + d, group + d + 1])
+    deltas = []
+    for h in range(heads):
+        rows = slice(h * tok, (h + 1) * tok)
+        part = jnp.sum(w_ref[rows, prev].astype(F32) * dp_ref[rows, prev], axis=1, keepdims=True)
+        deltas.append(own_delta[h] * own_scale[h] + part)
+    delta = jnp.concatenate(deltas, axis=0)
+
+    for first in firsts:
+        send_prev(0, first, key_terms(group + first))
+    for first in firsts:
+        keep_own(1, first, dot_nn(do_t[...], w_ref[:, pair(first)]))
+    send_own(1)
+    for first in firsts:
+        keep_own(0, first, key_terms(first))
     all_values = cat([values_of(b) for b in range(blocks)], 0)
     attended = dot_nn(w_ref[...], all_values).astype(BF16)
-    delta = jnp.sum(dos[...].astype(F32) * attended.astype(F32), axis=1, keepdims=True)
     for h in range(heads):
         att_ref[:, h * dim : (h + 1) * dim] = attended[h * tok : (h + 1) * tok]
     stores[0].start()
-
-    for first in firsts[::-1]:
-        send_own(1, first, dot_nn(do_t[...], w_ref[:, pair(first)]))
-    for first in firsts:
-        send_prev(0, first, key_terms(group + first))
-    for first in firsts[::-1]:
-        send_own(0, first, key_terms(first))
+    send_own(0)
 
     all_keys = cat([keys_of(b) for b in range(blocks)], 0)
-    gq = (dot_nn(w_ref[...], all_keys) * scale).astype(BF16)
+    gq = (dot_nn(ds_ref[...], all_keys) * scale).astype(BF16)
     for h in range(heads):
         gq_ref[:, h * dim : (h + 1) * dim] = gq[h * tok : (h + 1) * tok]
     stores[1].start()
@@ -308,9 +334,11 @@
             ((rows, keys), F32),
             ((rows, keys), F32),
             ((rows, keys), BF16),
+            ((rows, keys), BF16),
             ((2, group, dim, tok), BF16),
             ((2, group, dim, tok), BF16),
             ((2, group, dim, tok), BF16),
+            ((2, group, dim, tok), F32),
             ((2, dim, tok), F32),
             (wide, BF16),
             (wide, BF16),

time: 29.1 us -> 28 us (0.962); the launches traced: 28.7 us -> 27.9 us
  Pallas kernels: 28 us -> 27.2 us
    pallas_call x1, Pallas kernels: 26.1 us -> 25.3 us  [body(): pl.pallas_call(functools.partial(kernel, segments, group, heads, dim, tok...]
where the time goes in v5:
time: 28 us; the launch traced here: 27.9 us
  Pallas kernels  27.2 us (97%)
  between operations  0.64 us (2%)
    pallas_call x1, Pallas kernels, body(): pl.pallas_call(functools.partial(kernel, segments, group, heads, dim, tok...  25.3 us
    pallas_call x1, Pallas kernels, body(): pl.pallas_call(functools.partial(store_kernel, group), out_shape=[jax.Sha...  1.98 us

profile of v5, /device:TPU:1, one launch (start us, length us, event | category | flops | bytes accessed | tf_op | source)
XLA Modules:
  0.0 27.9 jit_solution(8411252907745970502)
XLA Ops:
  0.6 25.3 %window_attention.1 = (bf16[128,1024]{1,0:T(8,128)(2,1)}, bf16[128,1024]{1,0:T(8,128)(2,1)}, f32[2,128,128]{2,1,0:T(8,128)}, bf16[2,3,128,128]{3,2,1,0:T(8,128)(2,1)}) custom-call(bf16[128,1024]{1,0:T(8,128)(2,1)} %q_hbm.1, bf16[128,128]{1,0:T(8,128)(2,1)} %k_hbm.1, bf16[128,128]{1,0:T(8,128)(2,1)} %v_hbm.1, bf16[128,1024]{1,0:T(8,128)(2,1)} %do_hbm.1, ...), custom_call_target="tpu_custom_call" | custom-call | tf_op jit(solution)/shard_map/window_attention/pallas_call | solution.py:350
  25.9 2.0 %store_results.1 = (bf16[128,1024]{1,0:T(8,128)(2,1)}, bf16[128,1024]{1,0:T(8,128)(2,1)}, bf16[128,128]{1,0:T(8,128)(2,1)}, bf16[128,128]{1,0:T(8,128)(2,1)}) custom-call(bf16[128,1024]{1,0:T(8,128)(2,1)} %get-tuple-element.8.att_hbm, bf16[128,1024]{1,0:T(8,128)(2,1)} %get-tuple-element.9.gq_hbm, f32[2,128,128]{2,1,0:T(8,128)} %get-tuple-element.10.mine_hbm, ...), custom_call_target="tpu_custom_call" | custom-call | tf_op jit(solution)/shard_map/store_results/pallas_call | solution.py:364

commit v6 on v5

--- a/solution.py
+++ b/solution.py
@@ -153,9 +153,10 @@
 
     rate = scale * math.log2(math.e)
     own, prev = slice(0, group * tok), slice(group * tok, blocks * tok)
+    last = heads // 2 - 1
+    chunks = [slice(n * 2 * tok, (n + 1) * 2 * tok) for n in range(heads // 2)]
     own_top, own_sum = [], []
-    for h in range(heads):
-        rows = slice(h * tok, (h + 1) * tok)
+    for rows in chunks:
         s = s_ref[rows, own]
         top = jnp.max(s, axis=1, keepdims=True)
         e = jnp.exp2((s - top) * rate)
@@ -169,24 +170,8 @@
     for d in range(0, group, 2):
         grad_step([d, d + 1])
     own_delta = []
-    for h in range(heads):
-        rows = slice(h * tok, (h + 1) * tok)
+    for rows in chunks:
         own_delta.append(jnp.sum(s_ref[rows, own] * dp_ref[rows, own], axis=1, keepdims=True))
-
-    for d in range(0, group, 2):
-        k_forwards[d].wait_recv()
-        k_forwards[d + 1].wait_recv()
-        score_step([group + d, group + d + 1])
-    own_scale = []
-    for h in range(heads):
-        rows = slice(h * tok, (h + 1) * tok)
-        s = s_ref[rows, prev]
-        top = jnp.maximum(own_top[h], jnp.max(s, axis=1, keepdims=True))
-        e = jnp.exp2((s - top) * rate)
-        shrink = jnp.exp2((own_top[h] - top) * rate)
-        inv = 1.0 / (own_sum[h] * shrink + jnp.sum(e, axis=1, keepdims=True))
-        w_ref[rows, prev] = (e * inv).astype(BF16)
-        own_scale.append(shrink * inv)
 
     def prev_copy(part, first):
         return pltpu.make_async_remote_copy(
@@ -209,10 +194,11 @@
     def pair(first):
         return columns([first, first + 1])
 
-    def send_prev(part, first, total):
-        for n in range(2):
-            p_send[part, first + n] = total[:, n * tok : (n + 1) * tok].astype(BF16)
-        prev_copies[part, first].start()
+    def send_prev(part, total):
+        for first in firsts:
+            for d in (first, first + 1):
+                p_send[part, d] = total[:, d * tok : (d + 1) * tok].astype(BF16)
+            prev_copies[part, first].start()
 
     def send_own(part):
         for first in firsts[::-1]:
@@ -236,25 +222,47 @@
         ds_ref[:, cols] = ds
         return dot_nn(q_t[...], ds) * scale
 
-    for first in firsts:
-        send_prev(1, first, dot_nn(do_t[...], w_ref[:, pair(group + first)]))
-
-    for h in range(heads):
-        rows = slice(h * tok, (h + 1) * tok)
-        w_ref[rows, own] = (s_ref[rows, own] * own_scale[h]).astype(BF16)
-    for d in range(0, group, 2):
-        v_forwards[d].wait_recv()
-        v_forwards[d + 1].wait_recv()
-        grad_step([group + d, group + d + 1])
-    deltas = []
-    for h in range(heads):
-        rows = slice(h * tok, (h + 1) * tok)
-        part = jnp.sum(w_ref[rows, prev].astype(F32) * dp_ref[rows, prev], axis=1, keepdims=True)
-        deltas.append(own_delta[h] * own_scale[h] + part)
+    for copy in k_forwards:
+        copy.wait_recv()
+    prev_keys = cat([keys_of(group + d) for d in range(group)], 0)
+    own_scale, total = [], None
+    ready = dot_nt(qs[chunks[0], :], prev_keys)
+    for n, rows in enumerate(chunks):
+        s = ready + prev_bias
+        if n < last:
+            ready = dot_nt(qs[chunks[n + 1], :], prev_keys)
+        top = jnp.maximum(own_top[n], jnp.max(s, axis=1, keepdims=True))
+        e = jnp.exp2((s - top) * rate)
+        shrink = jnp.exp2((own_top[n] - top) * rate)
+        inv = 1.0 / (own_sum[n] * shrink + jnp.sum(e, axis=1, keepdims=True))
+        w = (e * inv).astype(BF16)
+        w_ref[rows, prev] = w
+        own_scale.append(shrink * inv)
+        term = dot_nn(do_t[:, rows], w)
+        total = term if total is None else total + term
+    send_prev(1, total)
+
+    for n, rows in enumerate(chunks):
+        w_ref[rows, own] = (s_ref[rows, own] * own_scale[n]).astype(BF16)
+    for copy in v_forwards:
+        copy.wait_recv()
+    prev_values = cat([values_of(group + d) for d in range(group)], 0)
+    deltas, total = [], None
+    ready = dot_nt(dos[chunks[0], :], prev_values)
+    for n, rows in enumerate(chunks):
+        dp = ready
+        if n < last:
+            ready = dot_nt(dos[chunks[n + 1], :], prev_values)
+        w = w_ref[rows, prev].astype(F32)
+        row_delta = own_delta[n] * own_scale[n] + jnp.sum(w * dp, axis=1, keepdims=True)
+        deltas.append(row_delta)
+        ds = (w * (dp - row_delta)).astype(BF16)
+        ds_ref[rows, prev] = ds
+        term = dot_nn(q_t[:, rows], ds)
+        total = term if total is None else total + term
+    send_prev(0, total * scale)
     delta = jnp.concatenate(deltas, axis=0)
 
-    for first in firsts:
-        send_prev(0, first, key_terms(group + first))
     for first in firsts:
         keep_own(1, first, dot_nn(do_t[...], w_ref[:, pair(first)]))
     send_own(1)
@@ -331,8 +339,8 @@
             ((rows, dim), BF16),
             ((dim, rows), BF16),
             ((dim, rows), BF16),
-            ((rows, keys), F32),
-            ((rows, keys), F32),
+            ((rows, group * tok), F32),
+            ((rows, group * tok), F32),
             ((rows, keys), BF16),
             ((rows, keys), BF16),
             ((2, group, dim, tok), BF16),

time: 28 us -> 27.7 us (0.989)
  Pallas kernels: 27.2 us -> 26.9 us
    pallas_call x1, Pallas kernels: 25.3 us -> 24.9 us  [body(): pl.pallas_call(functools.partial(kernel, segments, group, heads, dim, tok...]
where the time goes in v6:
time: 27.7 us; the launch traced here: 27.5 us
  Pallas kernels  26.9 us (97%)
  between operations  0.64 us (2%)
    pallas_call x1, Pallas kernels, body(): pl.pallas_call(functools.partial(kernel, segments, group, heads, dim, tok...  24.9 us
    pallas_call x1, Pallas kernels, body(): pl.pallas_call(functools.partial(store_kernel, group), out_shape=[jax.Sha...  1.98 us

profile of v6, /device:TPU:1, one launch (start us, length us, event | category | flops | bytes accessed | tf_op | source)
XLA Modules:
  0.0 27.5 jit_solution(2559042657897677745)
XLA Ops:
  0.6 24.9 %window_attention.1 = (bf16[128,1024]{1,0:T(8,128)(2,1)}, bf16[128,1024]{1,0:T(8,128)(2,1)}, f32[2,128,128]{2,1,0:T(8,128)}, bf16[2,3,128,128]{3,2,1,0:T(8,128)(2,1)}) custom-call(bf16[128,1024]{1,0:T(8,128)(2,1)} %q_hbm.1, bf16[128,128]{1,0:T(8,128)(2,1)} %k_hbm.1, bf16[128,128]{1,0:T(8,128)(2,1)} %v_hbm.1, bf16[128,1024]{1,0:T(8,128)(2,1)} %do_hbm.1, ...), custom_call_target="tpu_custom_call" | custom-call | tf_op jit(solution)/shard_map/window_attention/pallas_call | solution.py:358
  25.5 2.0 %store_results.1 = (bf16[128,1024]{1,0:T(8,128)(2,1)}, bf16[128,1024]{1,0:T(8,128)(2,1)}, bf16[128,128]{1,0:T(8,128)(2,1)}, bf16[128,128]{1,0:T(8,128)(2,1)}) custom-call(bf16[128,1024]{1,0:T(8,128)(2,1)} %get-tuple-element.8.att_hbm, bf16[128,1024]{1,0:T(8,128)(2,1)} %get-tuple-element.9.gq_hbm, f32[2,128,128]{2,1,0:T(8,128)} %get-tuple-element.10.mine_hbm, ...), custom_call_target="tpu_custom_call" | custom-call | tf_op jit(solution)/shard_map/store_results/pallas_call | solution.py:372

commit v7 on v6

--- a/solution.py
+++ b/solution.py
@@ -52,13 +52,12 @@
         pltpu.make_async_copy(g_mine.at[0], mine_hbm.at[0], out_sem.at[2]),
         pltpu.make_async_copy(g_mine.at[1], mine_hbm.at[1], out_sem.at[3]),
     ]
-    for load in loads:
-        load.start()
-
     barrier = pltpu.get_barrier_semaphore()
     partners = [(seg, lax.rem(me + d, group)) for d in range(1, group)] + [(nxt, me), (prv, me)]
     for partner in partners:
         pl.semaphore_signal(barrier, inc=1, device_id=partner, device_id_type=MESH)
+    for load in loads:
+        load.start()
 
     for load in loads[:3]:
         load.wait()
@@ -99,8 +98,6 @@
         dos[rows, :] = do_h
         q_t[:, rows] = q_h.astype(F32).T.astype(BF16)
         do_t[:, rows] = do_h.astype(F32).T.astype(BF16)
-    for d in others:
-        v_copies[d].start()
     v_forwards[0].start()
 
     pos_col = jnp.broadcast_to(pos.astype(F32), (tok, tok)).T
@@ -147,6 +144,8 @@
     for d in nearest:
         gather(k_own, k_ssem, k_rsem, d).wait_recv()
         forward(k_own, k_prev, kf_ssem, kf_rsem, d).start()
+    for d in others:
+        v_copies[d].start()
     score_step([1])
     for d in range(2, group, 2):
         score_step([d, d + 1])
@@ -244,6 +243,8 @@
 
     for n, rows in enumerate(chunks):
         w_ref[rows, own] = (s_ref[rows, own] * own_scale[n]).astype(BF16)
+    for first in firsts:
+        keep_own(1, first, dot_nn(do_t[...], w_ref[:, pair(first)]))
     for copy in v_forwards:
         copy.wait_recv()
     prev_values = cat([values_of(group + d) for d in range(group)], 0)
@@ -263,8 +264,6 @@
     send_prev(0, total * scale)
     delta = jnp.concatenate(deltas, axis=0)
 
-    for first in firsts:
-        keep_own(1, first, dot_nn(do_t[...], w_ref[:, pair(first)]))
     send_own(1)
     for first in firsts:
         keep_own(0, first, key_terms(first))

time: 27.7 us -> 29.2 us (1.054)
  Pallas kernels: 26.9 us -> 28.4 us
    pallas_call x1, Pallas kernels: 24.9 us -> 26.4 us  [body(): pl.pallas_call(functools.partial(kernel, segments, group, heads, dim, tok...]
where the time goes in v7:
time: 29.2 us; the launch traced here: 29.1 us
  Pallas kernels  28.4 us (97%)
  between operations  0.64 us (2%)
    pallas_call x1, Pallas kernels, body(): pl.pallas_call(functools.partial(kernel, segments, group, heads, dim, tok...  26.4 us
    pallas_call x1, Pallas kernels, body(): pl.pallas_call(functools.partial(store_kernel, group), out_shape=[jax.Sha...  1.98 us

profile of v7, /device:TPU:1, one launch (start us, length us, event | category | flops | bytes accessed | tf_op | source)
XLA Modules:
  0.0 29.1 jit_solution(11338571013524372957)
XLA Ops:
  0.6 26.4 %window_attention.1 = (bf16[128,1024]{1,0:T(8,128)(2,1)}, bf16[128,1024]{1,0:T(8,128)(2,1)}, f32[2,128,128]{2,1,0:T(8,128)}, bf16[2,3,128,128]{3,2,1,0:T(8,128)(2,1)}) custom-call(bf16[128,1024]{1,0:T(8,128)(2,1)} %q_hbm.1, bf16[128,128]{1,0:T(8,128)(2,1)} %k_hbm.1, bf16[128,128]{1,0:T(8,128)(2,1)} %v_hbm.1, bf16[128,1024]{1,0:T(8,128)(2,1)} %do_hbm.1, ...), custom_call_target="tpu_custom_call" | custom-call | tf_op jit(solution)/shard_map/window_attention/pallas_call | solution.py:357
  27.1 2.0 %store_results.1 = (bf16[128,1024]{1,0:T(8,128)(2,1)}, bf16[128,1024]{1,0:T(8,128)(2,1)}, bf16[128,128]{1,0:T(8,128)(2,1)}, bf16[128,128]{1,0:T(8,128)(2,1)}) custom-call(bf16[128,1024]{1,0:T(8,128)(2,1)} %get-tuple-element.8.att_hbm, bf16[128,1024]{1,0:T(8,128)(2,1)} %get-tuple-element.9.gq_hbm, f32[2,128,128]{2,1,0:T(8,128)} %get-tuple-element.10.mine_hbm, ...), custom_call_target="tpu_custom_call" | custom-call | tf_op jit(solution)/shard_map/store_results/pallas_call | solution.py:371
